TPU v7x, 256 devices: a whole 4x4x8 slice. The times are simulated.
256 devices in a mesh: req: 8 (over x, core), work: 32 (over z, y).
Axes of the slice: x: 4, y: 4, z: 8, core: 2. Of those that a mesh axis runs over, the one named last changes fastest.
Arguments:
- passage_query: bfloat16 [32768, 8192], P('work', 'req'), may hold values from -64 to 64
- passage_key_value: bfloat16 [2, 32768, 1024], P(None, 'work', 'req'), may hold values from -64 to 64
- passage_length: int32 [64], replicated, may hold values from 1 to 4, as said below
- passage_slot: int32 [64], replicated, may hold values from 0 to 63, each once
- cites: int32 [256, 4], P(('req', 'work')), may hold values from 0 to 63, all different within a row
- question_query: bfloat16 [32768, 8192], P(('req', 'work')), may hold values from -64 to 64
- question_key_value: bfloat16 [32768, 2, 1024], P(('req', 'work')), may hold values from -64 to 64
- question_length: int32 [256], P(('req', 'work')), may hold values from 1 to 128, as said below
Outputs:
- passage_output: bfloat16 [32768, 8192], P('work', 'req')
- question_output: bfloat16 [32768, 8192], P(('req', 'work'))
Inputs may be any that keep to these rules, and one draw needn't show every extreme that they name: `cites`: each row names 4 different passages and every passage is cited by some request. `passage_length`: some slot holds a passage of 4 blocks. `question_length`: some request has 128 question tokens.
All inputs are finite; a program needn't handle non-finite values.
Results may differ from a plain program's by a relative error of at most 0.0049.
Values may be sent and summed in bfloat16 or wider, within the bound.
No kernel may reach another device: no remote copies, remote signals or barrier semaphores. Data moves between devices by JAX's collectives and lax.ppermute only.
A program may use at most 128 MiB of HBM per device.

v0:
```python
import math

import jax
import jax.numpy as jnp
from jax import lax
from jax.sharding import PartitionSpec as P

QUERY_HEADS = 64
KEY_VALUE_HEADS = 8
HEAD_SIZE = 128
BLOCK = 128
CITED_PASSAGES = 4
QUESTION_LENGTH = 128
PASSAGE_ROWS = 512


def single_head_attention(query_matrix, key_matrix, value_matrix, visible_mask):
    scores = jnp.einsum(
        "qgd,pd->gqp", query_matrix, key_matrix, preferred_element_type=jnp.float32
    ) * (1.0 / math.sqrt(HEAD_SIZE))
    scores = jnp.where(visible_mask[None], scores, -jnp.inf)
    highest = jnp.max(scores, axis=-1, keepdims=True)
    raised = jnp.exp(scores - highest)
    weights = (raised / jnp.sum(raised, axis=-1, keepdims=True)).astype(jnp.bfloat16)
    return jnp.einsum("gqp,pd->qgd", weights, value_matrix, preferred_element_type=jnp.float32)


def every_head_output(query_matrix, key_matrix, value_matrix, visible_mask):

    def one_head(current_head):
        return single_head_attention(
            lax.dynamic_index_in_dim(query_matrix, current_head, 1, keepdims=False),
            lax.dynamic_index_in_dim(key_matrix, current_head, 1, keepdims=False),
            lax.dynamic_index_in_dim(value_matrix, current_head, 1, keepdims=False),
            visible_mask,
        )

    head_output = lax.map(one_head, jnp.arange(key_matrix.shape[1]))
    return jnp.transpose(head_output, (1, 0, 2, 3))


def causal_slot(query_matrix, key_matrix, value_matrix, blocks):
    kv_heads = key_matrix.shape[1] // HEAD_SIZE
    query_group_size = QUERY_HEADS // KEY_VALUE_HEADS
    position = jnp.arange(PASSAGE_ROWS)
    visible_mask = position[None, :] <= position[:, None]
    head_output = every_head_output(
        query_matrix.reshape(PASSAGE_ROWS, kv_heads, query_group_size, HEAD_SIZE),
        key_matrix.reshape(PASSAGE_ROWS, kv_heads, HEAD_SIZE),
        value_matrix.reshape(PASSAGE_ROWS, kv_heads, HEAD_SIZE),
        visible_mask,
    )
    living = position < blocks * BLOCK
    return jnp.where(living[:, None], head_output.reshape(PASSAGE_ROWS, -1), 0.0).astype(
        jnp.bfloat16
    )


def slot_lookup(cited_ids, lookup_table):
    matches = cited_ids[..., None] == jnp.arange(lookup_table.shape[0])
    return jnp.sum(jnp.where(matches, lookup_table, 0), axis=-1)


def answer(query_matrix, passage_own_rows, referenced_rows, referenced_blocks, lengths):
    request_count = lengths.shape[0]
    kv_heads = passage_own_rows.shape[2] // HEAD_SIZE
    query_group_size = QUERY_HEADS // KEY_VALUE_HEADS

    def one_request(request_index):
        blocks = lax.dynamic_index_in_dim(referenced_blocks, request_index, 0, keepdims=False)
        length = lax.dynamic_index_in_dim(lengths, request_index, 0, keepdims=False)
        key_matrix = jnp.concatenate(
            [referenced_rows[0].reshape(CITED_PASSAGES * PASSAGE_ROWS, -1), passage_own_rows[:, 0]],
            axis=0,
        )
        value_matrix = jnp.concatenate(
            [referenced_rows[1].reshape(CITED_PASSAGES * PASSAGE_ROWS, -1), passage_own_rows[:, 1]],
            axis=0,
        )
        inner = jnp.arange(CITED_PASSAGES * PASSAGE_ROWS) % PASSAGE_ROWS
        owner = jnp.arange(CITED_PASSAGES * PASSAGE_ROWS) // PASSAGE_ROWS
        row_blocks = jnp.sum(
            jnp.where(owner[:, None] == jnp.arange(CITED_PASSAGES)[None, :], blocks[None, :], 0),
            axis=1,
        )
        passage_ok = inner < row_blocks * BLOCK
        position = jnp.arange(QUESTION_LENGTH)
        own_ok = position[None, :] <= position[:, None]
        visible_mask = jnp.concatenate(
            [
                jnp.broadcast_to(
                    passage_ok[None, :], (QUESTION_LENGTH, CITED_PASSAGES * PASSAGE_ROWS)
                ),
                own_ok,
            ],
            axis=1,
        )
        head_output = every_head_output(
            query_matrix.reshape(QUESTION_LENGTH, kv_heads, query_group_size, HEAD_SIZE),
            key_matrix.reshape(-1, kv_heads, HEAD_SIZE),
            value_matrix.reshape(-1, kv_heads, HEAD_SIZE),
            visible_mask,
        )
        living = position < length
        return jnp.where(living[:, None], head_output.reshape(QUESTION_LENGTH, -1), 0.0).astype(
            jnp.bfloat16
        )

    output = lax.map(one_request, jnp.arange(request_count))
    return output.reshape(request_count * QUESTION_LENGTH, -1)


def body(
    passage_query,
    passage_key_value,
    passage_length,
    passage_slot,
    cites,
    question_query,
    question_key_value,
    question_length,
):
    all_keys = lax.all_gather(passage_key_value, "work", axis=1, tiled=True)
    saved_values = all_keys.reshape(2, -1, PASSAGE_ROWS, all_keys.shape[2])
    column = lax.all_gather(cites, "req", axis=0, tiled=True)
    picked = jnp.take(saved_values, slot_lookup(column, passage_slot).reshape(-1), axis=1)
    arrived = lax.all_to_all(picked, "req", split_axis=1, concat_axis=3, tiled=True)
    my_slots = slot_lookup(cites, passage_slot)
    question_output = answer(
        question_query,
        question_key_value,
        arrived,
        slot_lookup(my_slots, passage_length),
        question_length,
    )
    worker = lax.axis_index("work")
    slot_total = passage_query.shape[0] // PASSAGE_ROWS
    my_blocks = lax.dynamic_slice_in_dim(passage_length, worker * slot_total, slot_total)
    pieces = []
    for slot_index in range(slot_total):
        lower = slot_index * PASSAGE_ROWS
        upper = lower + PASSAGE_ROWS
        pieces.append(
            causal_slot(
                passage_query[lower:upper],
                passage_key_value[0, lower:upper],
                passage_key_value[1, lower:upper],
                my_blocks[slot_index],
            )
        )
    passage_output = jnp.concatenate(pieces, axis=0)
    return (passage_output, question_output)


def solution(mesh):
    return jax.shard_map(
        body,
        mesh=mesh,
        in_specs=(
            P("work", "req"),
            P(None, "work", "req"),
            P(),
            P(),
            P(("req", "work"), None),
            P(("req", "work"), None),
            P(("req", "work"), None, None),
            P(("req", "work")),
        ),
        out_specs=(P("work", "req"), P(("req", "work"), None)),
        check_vma=False,
    )
```

profile of v0, /device:TPU:1, one launch (start us, length us, event | category | flops | bytes accessed | tf_op | source)
XLA Modules:
  0.0 409.2 jit_solution(1018482690392673808)
XLA Ops:
  7.2 0.7 all-gather.3.cloned.1.call-update
  7.9 12.0 %all-gather = s32[8,1,4]{2,1,0:T(1,128)S(1)} all-gather(s32[1,1,4]{2,1,0:T(1,128)} %bitcast.176), channel_id=1, replica_groups=mesh['req'=8,'work'=32] {'req'}, dimensions={0}, use_global_device_ids=true | all-gather | bytes 144 | tf_op jit(solution)/shard_map/all_gather | solution.py:125
  19.9 0.1 copy.76
  19.9 0.9 select_reduce_fusion.1
  20.8 0.1 copy.77
  20.9 0.1 reshape.267
  21.1 133.5 %all-gather.3.cloned.1.call-done = bf16[2,32768,128]{2,1,0:T(8,128)(2,1)} async-done(((bf16[2,1024,128]{2,1,0:T(8,128)(2,1)}), bf16[2,32768,128]{2,1,0:T(8,128)(2,1)}) %all-gather.3.cloned.1.call-update) | async-done | bytes 16777232 | tf_op jit(solution)/shard_map/all_gather | solution.py:123
  154.6 10.8 %gather_fusion = bf16[32,2,512,128]{3,2,1,0:T(8,128)(2,1)} fusion(bf16[2,64,512,128]{3,2,1,0:T(8,128)(2,1)} %bitcast.166, s32[1024]{0:T(1024)S(1)} %pad_clamp_fusion), kind=kCustom, calls=%fused_computation | custom fusion | bytes 16777344 | tf_op jit(solution)/shard_map/jit(_take)/gather | solution.py:126
  165.4 7.5 %select_bitcast_fusion = bf16[2,32,512,128]{3,2,0,1:T(8,128)(2,1)} fusion(bf16[32,2,512,128]{3,2,1,0:T(8,128)(2,1)} %gather_fusion, pred[32]{0:T(512)(128)(4,1)S(1)} %compare_and_fusion), kind=kLoop, calls=%fused_computation.37 | loop fusion | flops 4194304 | bytes 16777248 | tf_op jit(solution)/shard_map/jit(_take)/select_n | solution.py:126
  172.9 6.1 %all-to-all-start = ((bf16[2,32,512,128]{3,2,0,1:T(8,128)(2,1)}), bf16[2,32,512,128]{3,2,0,1:T(8,128)(2,1)}, u32[]{:S(2)}, u32[]{:S(2)}) async-start(bf16[2,32,512,128]{3,2,0,1:T(8,128)(2,1)} %select_bitcast_fusion), calls=%async_computation | async-start | bytes 16777216 | tf_op jit(solution)/shard_map/all_to_all | solution.py:127
  179.8 0.6 fusion.110
  181.6 1.5 fusion.109
  183.2 1.3 copy.99
  184.4 0.2 copy.83
  184.6 0.4 copy.81
  185.1 2.5 copy.84
  187.6 1.7 fusion.108
  189.3 1.3 copy.96
  190.7 0.5 copy.98
  191.3 4.9 %fusion.111 = (f32[8,512]{1,0:T(8,128)S(1)}, f32[8,512,512]{1,2,0:T(8,128)}) fusion(pred[512,512]{0,1:T(8,128)(4,1)S(1)} %iota_compare_fusion, bf16[512,8,128]{0,2,1:T(8,128)(2,1)S(1)} %bitcast.172, bf16[2,1024,128]{2,1,0:T(8,128)(2,1)S(1)} %copy-done.4), kind=kOutput, calls=%fused_computation.113 | convolution fusion | flops 545260032 | bytes 9846784 | tf_op jit(solution)/shard_map/while/body/eval_jaxpr/sub | solution.py:23
  196.3 5.2 %fusion.58 = bf16[8,512,128]{1,2,0:T(8,128)(2,1)} fusion(f32[8,512,512]{1,2,0:T(8,128)} %get-tuple-element.141, f32[8,512]{1,0:T(8,128)S(1)} %get-tuple-element.140, bf16[2,1024,128]{2,1,0:T(8,128)(2,1)S(1)} %copy-done.4), kind=kOutput, calls=%fused_computation.52 | convolution fusion | flops 541065216 | bytes 9584640 | tf_op jit(solution)/shard_map/while/body/eval_jaxpr/gqp,pd->qgd/dot_general | solution.py:25
  201.5 1.5 copy.75
  203.0 4.9 %fusion.116 = (f32[8,512]{1,0:T(8,128)S(1)}, f32[8,512,512]{1,2,0:T(8,128)}) fusion(pred[512,512]{0,1:T(8,128)(4,1)S(1)} %iota_compare_fusion, bf16[512,8,128]{0,2,1:T(8,128)(2,1)S(1)} %bitcast.171, bf16[2,1024,128]{2,1,0:T(8,128)(2,1)S(1)} %copy-done.4), kind=kOutput, calls=%fused_computation.114 | convolution fusion | flops 545260032 | bytes 9846784 | tf_op jit(solution)/shard_map/while/body/eval_jaxpr/sub | solution.py:23
  207.9 5.1 %fusion.57 = bf16[8,512,128]{1,2,0:T(8,128)(2,1)} fusion(f32[8,512,512]{1,2,0:T(8,128)} %get-tuple-element.143, f32[8,512]{1,0:T(8,128)S(1)} %get-tuple-element.142, bf16[2,1024,128]{2,1,0:T(8,128)(2,1)S(1)} %copy-done.4), kind=kOutput, calls=%fused_computation.51 | convolution fusion | flops 541065216 | bytes 9584640 | tf_op jit(solution)/shard_map/while/body/eval_jaxpr/gqp,pd->qgd/dot_general | solution.py:25
  213.0 1.5 copy.70
  214.6 0.2 select_reduce_fusion.3
  214.7 0.2 select_reduce_fusion.2
  214.9 0.1 select_reduce_fusion
  215.1 0.4 select_convert_fusion.1
  215.6 1.5 pad_maximum_fusion.2
  217.1 2.0 pad_add_fusion
  219.1 53.8 %all-to-all-done = bf16[2,32,512,128]{3,2,0,1:T(8,128)(2,1)} async-done(((bf16[2,32,512,128]{3,2,0,1:T(8,128)(2,1)}), bf16[2,32,512,128]{3,2,0,1:T(8,128)(2,1)}, u32[]{:S(2)}, u32[]{:S(2)}) %all-to-all-start) | async-done | bytes 8388640 | tf_op jit(solution)/shard_map/all_to_all | solution.py:127
  272.9 7.6 %copy.79 = bf16[2,32,512,128]{3,2,1,0:T(8,128)(2,1)} copy(bf16[2,32,512,128]{3,2,0,1:T(8,128)(2,1)} %all-to-all-done) | data formatting | bytes 16777216 | tf_op jit(solution)/shard_map/all_to_all | solution.py:127
  280.5 5.9 %fusion.107 = (bf16[1,4,512,8,128]{4,2,1,3,0:T(8,128)(2,1)}, bf16[1,4,512,8,128]{4,2,1,3,0:T(8,128)(2,1)}) fusion(bf16[2,4,512,8,128]{4,2,1,3,0:T(8,128)(2,1)} %bitcast.163), kind=kLoop, calls=%fused_computation.109 | loop fusion | bytes 16777216 | tf_op jit(solution)/shard_map/while/body/eval_jaxpr/slice | solution.py:73
  286.4 6.6 %copy.92 = bf16[2048,8,128]{0,2,1:T(8,128)(2,1)} copy(bf16[2048,8,128]{2,0,1:T(8,128)(2,1)} %bitcast.165) | data formatting | bytes 8388608 | tf_op jit(solution)/shard_map/while/body/eval_jaxpr/concatenate | solution.py:76
  293.0 4.7 %pad_maximum_fusion.1 = bf16[2176,8,128]{2,0,1:T(8,128)(2,1)} fusion(bf16[128,8,128]{2,0,1:T(8,128)(2,1)S(1)} %copy.83, bf16[2048,8,128]{2,0,1:T(8,128)(2,1)} %bitcast.164), kind=kLoop, calls=%fused_computation.45 | loop fusion | flops 8912896 | bytes 8912896 | tf_op jit(solution)/shard_map/while/body/eval_jaxpr/concatenate | solution.py:72
  297.7 2.6 pad_maximum_fusion
  300.2 97.4 %while.13 = (s32[]{:T(128)}, bf16[8,128,8,128]{1,3,2,0:T(8,128)(2,1)}, s32[8]{0:T(128)S(1)}, bf16[2176,8,128]{0,2,1:T(8,128)(2,1)}, pred[128,2176]{0,1:T(8,128)(...) while((s32[]{:T(128)}, ...), condition=%wide.region_11.12_spmd, body=%wide.region_8.11_spmd.sunk | while | flops 1731335424 | bytes 3288219 | solution.py:38
  300.2 0.6 dynamic_slice.93
  302.4 4.0 fusion.137
  306.4 6.0 %fusion.138 = bf16[8,128,8,128]{1,3,2,0:T(8,128)(2,1)} fusion(bf16[8,128,8,128]{1,3,2,0:T(8,128)(2,1)} %get-tuple-element.200, s32[]{:T(128)S(6)} %copy.103, f32[8,128]{1,0:T(8,128)S(1)} %fusion.137, bf16[2176,8,128]{0,2,1:T(8,128)(2,1)} %get-tuple-element.212, s32[]{:T(128)S(6)} %select_n.195, pred[128,2176]{0,1:T(8,128)(4,1)S(1)} %get-tuple-element.213, ...), kind=kOutput, calls=%fused_computation.12.clone.1 | convolution fusion | flops 1151995008 | bytes 2185216 | tf_op jit(solution)/shard_map/while/body/eval_jaxpr/while/body/eval_jaxpr/gqp,pd->qgd/dot_general | solution.py:25
  312.4 0.6 dynamic_slice.93
  314.6 4.0 fusion.137
  318.6 6.0 %fusion.138 = bf16[8,128,8,128]{1,3,2,0:T(8,128)(2,1)} fusion(bf16[8,128,8,128]{1,3,2,0:T(8,128)(2,1)} %get-tuple-element.200, s32[]{:T(128)S(6)} %copy.103, f32[8,128]{1,0:T(8,128)S(1)} %fusion.137, bf16[2176,8,128]{0,2,1:T(8,128)(2,1)} %get-tuple-element.212, s32[]{:T(128)S(6)} %select_n.195, pred[128,2176]{0,1:T(8,128)(4,1)S(1)} %get-tuple-element.213, ...), kind=kOutput, calls=%fused_computation.12.clone.1 | convolution fusion | flops 1151995008 | bytes 2185216 | tf_op jit(solution)/shard_map/while/body/eval_jaxpr/while/body/eval_jaxpr/gqp,pd->qgd/dot_general | solution.py:25
  324.6 0.6 dynamic_slice.93
  326.8 4.0 fusion.137
  330.8 6.0 %fusion.138 = bf16[8,128,8,128]{1,3,2,0:T(8,128)(2,1)} fusion(bf16[8,128,8,128]{1,3,2,0:T(8,128)(2,1)} %get-tuple-element.200, s32[]{:T(128)S(6)} %copy.103, f32[8,128]{1,0:T(8,128)S(1)} %fusion.137, bf16[2176,8,128]{0,2,1:T(8,128)(2,1)} %get-tuple-element.212, s32[]{:T(128)S(6)} %select_n.195, pred[128,2176]{0,1:T(8,128)(4,1)S(1)} %get-tuple-element.213, ...), kind=kOutput, calls=%fused_computation.12.clone.1 | convolution fusion | flops 1151995008 | bytes 2185216 | tf_op jit(solution)/shard_map/while/body/eval_jaxpr/while/body/eval_jaxpr/gqp,pd->qgd/dot_general | solution.py:25
  336.8 0.6 dynamic_slice.93
  339.0 4.0 fusion.137
  343.0 6.0 %fusion.138 = bf16[8,128,8,128]{1,3,2,0:T(8,128)(2,1)} fusion(bf16[8,128,8,128]{1,3,2,0:T(8,128)(2,1)} %get-tuple-element.200, s32[]{:T(128)S(6)} %copy.103, f32[8,128]{1,0:T(8,128)S(1)} %fusion.137, bf16[2176,8,128]{0,2,1:T(8,128)(2,1)} %get-tuple-element.212, s32[]{:T(128)S(6)} %select_n.195, pred[128,2176]{0,1:T(8,128)(4,1)S(1)} %get-tuple-element.213, ...), kind=kOutput, calls=%fused_computation.12.clone.1 | convolution fusion | flops 1151995008 | bytes 2185216 | tf_op jit(solution)/shard_map/while/body/eval_jaxpr/while/body/eval_jaxpr/gqp,pd->qgd/dot_general | solution.py:25
  349.0 0.6 dynamic_slice.93
  351.2 4.0 fusion.137
  355.1 6.0 %fusion.138 = bf16[8,128,8,128]{1,3,2,0:T(8,128)(2,1)} fusion(bf16[8,128,8,128]{1,3,2,0:T(8,128)(2,1)} %get-tuple-element.200, s32[]{:T(128)S(6)} %copy.103, f32[8,128]{1,0:T(8,128)S(1)} %fusion.137, bf16[2176,8,128]{0,2,1:T(8,128)(2,1)} %get-tuple-element.212, s32[]{:T(128)S(6)} %select_n.195, pred[128,2176]{0,1:T(8,128)(4,1)S(1)} %get-tuple-element.213, ...), kind=kOutput, calls=%fused_computation.12.clone.1 | convolution fusion | flops 1151995008 | bytes 2185216 | tf_op jit(solution)/shard_map/while/body/eval_jaxpr/while/body/eval_jaxpr/gqp,pd->qgd/dot_general | solution.py:25
  361.1 0.6 dynamic_slice.93
  363.3 4.0 fusion.137
  367.3 6.0 %fusion.138 = bf16[8,128,8,128]{1,3,2,0:T(8,128)(2,1)} fusion(bf16[8,128,8,128]{1,3,2,0:T(8,128)(2,1)} %get-tuple-element.200, s32[]{:T(128)S(6)} %copy.103, f32[8,128]{1,0:T(8,128)S(1)} %fusion.137, bf16[2176,8,128]{0,2,1:T(8,128)(2,1)} %get-tuple-element.212, s32[]{:T(128)S(6)} %select_n.195, pred[128,2176]{0,1:T(8,128)(4,1)S(1)} %get-tuple-element.213, ...), kind=kOutput, calls=%fused_computation.12.clone.1 | convolution fusion | flops 1151995008 | bytes 2185216 | tf_op jit(solution)/shard_map/while/body/eval_jaxpr/while/body/eval_jaxpr/gqp,pd->qgd/dot_general | solution.py:25
  373.3 0.6 dynamic_slice.93
  375.5 4.0 fusion.137
  379.5 6.0 %fusion.138 = bf16[8,128,8,128]{1,3,2,0:T(8,128)(2,1)} fusion(bf16[8,128,8,128]{1,3,2,0:T(8,128)(2,1)} %get-tuple-element.200, s32[]{:T(128)S(6)} %copy.103, f32[8,128]{1,0:T(8,128)S(1)} %fusion.137, bf16[2176,8,128]{0,2,1:T(8,128)(2,1)} %get-tuple-element.212, s32[]{:T(128)S(6)} %select_n.195, pred[128,2176]{0,1:T(8,128)(4,1)S(1)} %get-tuple-element.213, ...), kind=kOutput, calls=%fused_computation.12.clone.1 | convolution fusion | flops 1151995008 | bytes 2185216 | tf_op jit(solution)/shard_map/while/body/eval_jaxpr/while/body/eval_jaxpr/gqp,pd->qgd/dot_general | solution.py:25
  385.5 0.6 dynamic_slice.93
  387.7 4.0 fusion.137
  391.7 6.0 %fusion.138 = bf16[8,128,8,128]{1,3,2,0:T(8,128)(2,1)} fusion(bf16[8,128,8,128]{1,3,2,0:T(8,128)(2,1)} %get-tuple-element.200, s32[]{:T(128)S(6)} %copy.103, f32[8,128]{1,0:T(8,128)S(1)} %fusion.137, bf16[2176,8,128]{0,2,1:T(8,128)(2,1)} %get-tuple-element.212, s32[]{:T(128)S(6)} %select_n.195, pred[128,2176]{0,1:T(8,128)(4,1)S(1)} %get-tuple-element.213, ...), kind=kOutput, calls=%fused_computation.12.clone.1 | convolution fusion | flops 1151995008 | bytes 2185216 | tf_op jit(solution)/shard_map/while/body/eval_jaxpr/while/body/eval_jaxpr/gqp,pd->qgd/dot_general | solution.py:25
  397.7 2.9 copy.93
  400.6 1.8 select_convert_fusion
  (32 shorter events, 0.4 us)
Async XLA Ops:
  7.2 147.5 %all-gather.3.cloned.1.call-start = ((), (), s32[]{:S(2)}) async-start(), calls=%async_computation.1 | async-start | bytes 17301504 | tf_op jit(solution)/shard_map/all_gather | solution.py:123
  172.9 6.8 %copy-start.7 = (s32[64]{0:T(128)S(1)}, s32[64]{0:T(128)}, u32[]{:S(2)}) copy-start(s32[64]{0:T(128)} %param.12) | copy-start | bytes 772
  172.9 8.8 %copy-start.2 = (bf16[128,2,1024]{2,1,0:T(2,128)(2,1)S(1)}, bf16[128,2,1024]{2,1,0:T(2,128)(2,1)}, u32[]{:S(2)}) copy-start(bf16[128,2,1024]{2,1,0:T(2,128)(2,1)} %param.16) | copy-start | bytes 1572868
  172.9 12.2 %copy-start.1 = (bf16[128,8192]{1,0:T(8,128)(2,1)S(1)}, bf16[128,8192]{1,0:T(8,128)(2,1)}, u32[]{:S(2)}) copy-start(bf16[128,8192]{1,0:T(8,128)(2,1)} %param.15) | copy-start | bytes 6291460
  172.9 100.0 %all-to-all-start = ((bf16[2,32,512,128]{3,2,0,1:T(8,128)(2,1)}), bf16[2,32,512,128]{3,2,0,1:T(8,128)(2,1)}, u32[]{:S(2)}, u32[]{:S(2)}) async-start(bf16[2,32,512,128]{3,2,0,1:T(8,128)(2,1)} %select_bitcast_fusion), calls=%async_computation | async-start | bytes 16777216 | tf_op jit(solution)/shard_map/all_to_all | solution.py:127
  185.1 6.2 %copy-start.4 = (bf16[2,1024,128]{2,1,0:T(8,128)(2,1)S(1)}, bf16[2,1024,128]{2,1,0:T(8,128)(2,1)}, u32[]{:S(2)}) copy-start(bf16[2,1024,128]{2,1,0:T(8,128)(2,1)} %param.11) | copy-start | bytes 1572868
  196.3 6.7 %copy-start.3 = (bf16[512,1024]{0,1:T(8,128)(2,1)S(1)}, bf16[512,1024]{0,1:T(8,128)(2,1)}, u32[]{:S(2)}) copy-start(bf16[512,1024]{0,1:T(8,128)(2,1)} %copy.96) | copy-start | bytes 3145732
  207.9 6.7 %copy-start.5 = (s32[64]{0:T(128)S(1)}, s32[64]{0:T(128)}, u32[]{:S(2)}) copy-start(s32[64]{0:T(128)} %param.13) | copy-start | bytes 772
  207.9 6.7 %copy-start.6 = (s32[1,4]{1,0:T(1,128)S(1)}, s32[1,4]{1,0:T(1,128)}, u32[]{:S(2)}) copy-start(s32[1,4]{1,0:T(1,128)} %param.14) | copy-start | bytes 52
  293.0 4.7 %copy-start = (bf16[2048,8,128]{0,2,1:T(8,128)(2,1)S(1)}, bf16[2048,8,128]{0,2,1:T(8,128)(2,1)}, u32[]{:S(2)}) copy-start(bf16[2048,8,128]{0,2,1:T(8,128)(2,1)} %copy.92) | copy-start | bytes 12582916
Sparse Core Ops, SparseCore 0:
  10.6 143.9 all-gather.2
where the time goes:
time: 410 us; the launch traced here: 409 us
  waiting for transfers between devices  188 us (46%)
  matrix products  100 us (24%)
  local copies, waits for them, and re-layouts  51.7 us (13%)
  other arithmetic  21.9 us (5%)
  between operations  16.2 us (4%)
  loops' own time  13.2 us (3%)
  blocking collectives  12 us (3%)
  starting transfers between devices  6.18 us (2%)
    all_gather x1, waiting for transfers between devices, body(): all_keys = lax.all_gather(passage_key_value, 'work', axis=1, tiled=True)  134 us
    dot_general x10, matrix products, single_head_attention(): jnp.einsum('gqp,pd->qgd', weights, value_matrix, preferred_element_type=j...  58.3 us
    all_to_all x1, waiting for transfers between devices, body(): lax.all_to_all(picked, 'req', split_axis=1, concat_axis=3, tiled=True)  53.8 us
    sub x10, matrix products, single_head_attention(): raised = jnp.exp(scores - highest)  41.7 us
    another operation x1, loops' own time, every_head_output(): head_output = lax.map(one_head, jnp.arange(key_matrix.shape[1]))  13.2 us
    all_gather x1, blocking collectives, body(): column = lax.all_gather(cites, 'req', axis=0, tiled=True)  12 us
    gather x1, local copies, waits for them, and re-layouts, body(): jnp.take(saved_values, slot_lookup(column, passage_slot).reshape(-1), axi...  10.8 us
  transfers between devices with their start and end apart: 2, of which 2 were waited for; matrix products, arithmetic and copies ran while one was open for 10% of the time, Pallas kernels for 0%

commit v1 on v0

v1 whole, which is shorter than its diff:
```python
import math

import jax
import jax.numpy as jnp
from jax import lax
from jax.experimental import pallas as pl
from jax.experimental.pallas import tpu as pltpu
from jax.sharding import PartitionSpec as P

QUERY_HEADS = 64
KEY_VALUE_HEADS = 8
GROUP = QUERY_HEADS // KEY_VALUE_HEADS
HEAD_SIZE = 128
BLOCK = 128
PBLK = 4
CITED_PASSAGES = 4
QUESTION_LENGTH = 128
PASSAGE_ROWS = 512
SCALE = math.log2(math.e) / math.sqrt(HEAD_SIZE)
LOW = -1e30
TILE = 32
MOST = CITED_PASSAGES * PBLK
DOT_NT = (((1,), (1,)), ((), ()))


def stack_heads(ref_rows):
    return jnp.concatenate(
        [ref_rows[:, h * HEAD_SIZE : (h + 1) * HEAD_SIZE] for h in range(GROUP)], axis=0
    )


def with_ones(values):
    return jnp.concatenate([values, jnp.ones_like(values)], axis=1)


def passage_kernel(blocks_ref, q_ref, kv_ref, out_ref):
    slot = pl.program_id(0)
    blocks = blocks_ref[slot]
    rows = GROUP * BLOCK
    row = lax.broadcasted_iota(jnp.int32, (rows, BLOCK), 0) % BLOCK
    column = lax.broadcasted_iota(jnp.int32, (rows, BLOCK), 1)
    causal = column <= row
    for i in range(PBLK):
        place = slice(i * BLOCK, (i + 1) * BLOCK)

        @pl.when(i < blocks)
        def _():
            q = stack_heads(q_ref[place, :])
            k = kv_ref[0, : (i + 1) * BLOCK, :]
            v = with_ones(kv_ref[1, : (i + 1) * BLOCK, :])
            s = lax.dot_general(q, k, DOT_NT, preferred_element_type=jnp.float32)
            last = jnp.where(causal, s[:, i * BLOCK :], LOW)
            s = last if i == 0 else jnp.concatenate([s[:, : i * BLOCK], last], axis=1)
            m = jnp.max(s, axis=1, keepdims=True)
            p = jnp.exp2((s - m) * SCALE).astype(jnp.bfloat16)
            o = jnp.dot(p, v, preferred_element_type=jnp.float32)
            o = (o[:, :HEAD_SIZE] / o[:, HEAD_SIZE:]).astype(jnp.bfloat16)
            for h in range(GROUP):
                out_ref[place, h * HEAD_SIZE : (h + 1) * HEAD_SIZE] = o[h * BLOCK : (h + 1) * BLOCK]

        @pl.when(i >= blocks)
        def _():
            out_ref[place, :] = jnp.zeros((BLOCK, GROUP * HEAD_SIZE), jnp.bfloat16)


def passage_attention(blocks, query, key_value):
    slots = query.shape[0] // PASSAGE_ROWS
    width = GROUP * HEAD_SIZE
    return pl.pallas_call(
        passage_kernel,
        out_shape=jax.ShapeDtypeStruct(query.shape, jnp.bfloat16),
        grid_spec=pltpu.PrefetchScalarGridSpec(
            num_scalar_prefetch=1,
            grid=(slots,),
            in_specs=[
                pl.BlockSpec((PASSAGE_ROWS, width), lambda s, b: (s, 0)),
                pl.BlockSpec((2, PASSAGE_ROWS, HEAD_SIZE), lambda s, b: (0, s, 0)),
            ],
            out_specs=pl.BlockSpec((PASSAGE_ROWS, width), lambda s, b: (s, 0)),
        ),
        compiler_params=pltpu.CompilerParams(vmem_limit_bytes=40 * 1024 * 1024),
        cost_estimate=pl.CostEstimate(
            flops=slots * 4 * 1024 * 512 * 512, bytes_accessed=5 * 1024 * 1024, transcendentals=0
        ),
    )(blocks, query, key_value)


def question_kernel(table_ref, count_ref, length_ref, q_ref, own_ref, kv_ref, out_ref, store, sems):
    request = pl.program_id(0)

    @pl.when(request == 0)
    def _():
        copies = [
            pltpu.make_async_copy(kv_ref.at[part], store.at[part], sems.at[part]) for part in range(2)
        ]
        for copy in copies:
            copy.start()
        for copy in copies:
            copy.wait()

    length = length_ref[request]
    count = count_ref[request]
    out_ref[...] = jnp.zeros_like(out_ref)
    rows = GROUP * TILE
    row = lax.broadcasted_iota(jnp.int32, (rows, BLOCK), 0) % TILE
    column = lax.broadcasted_iota(jnp.int32, (rows, BLOCK), 1)

    def attend(cited):
        places = [table_ref[request * (MOST + 1) + i] for i in range(cited)]
        extra = jnp.where(count < cited, LOW, 0.0)

        def tile_step(tile, carry):
            first = pl.multiple_of(tile * TILE, TILE)
            q = stack_heads(q_ref[0, pl.ds(first, TILE), :])
            k = jnp.concatenate([own_ref[0, 0]] + [store[0, at] for at in places], axis=0)
            v = jnp.concatenate([own_ref[0, 1]] + [store[1, at] for at in places], axis=0)
            s = lax.dot_general(q, k, DOT_NT, preferred_element_type=jnp.float32)
            s = jnp.concatenate(
                [
                    jnp.where(column <= row + first, s[:, :BLOCK], LOW),
                    s[:, BLOCK:-BLOCK],
                    s[:, -BLOCK:] + extra,
                ],
                axis=1,
            )
            m = jnp.max(s, axis=1, keepdims=True)
            p = jnp.exp2((s - m) * SCALE).astype(jnp.bfloat16)
            o = jnp.dot(p, with_ones(v), preferred_element_type=jnp.float32)
            o = o[:, :HEAD_SIZE] / o[:, HEAD_SIZE:]
            o = jnp.where(row + first < length, o, 0.0).astype(jnp.bfloat16)
            for h in range(GROUP):
                out_ref[0, pl.ds(first, TILE), h * HEAD_SIZE : (h + 1) * HEAD_SIZE] = o[
                    h * TILE : (h + 1) * TILE
                ]
            return carry

        lax.fori_loop(0, (length + TILE - 1) // TILE, tile_step, 0)

    for cited in range(CITED_PASSAGES + 1, MOST + 2, 2):
        pl.when((count + 1) // 2 * 2 + 1 - (count % 2) * 2 == cited)(lambda cited=cited: attend(cited))


def question_attention(table, count, length, query, own, key_value):
    requests, rows, width = query.shape
    return pl.pallas_call(
        question_kernel,
        out_shape=jax.ShapeDtypeStruct(query.shape, jnp.bfloat16),
        grid_spec=pltpu.PrefetchScalarGridSpec(
            num_scalar_prefetch=3,
            grid=(requests,),
            in_specs=[
                pl.BlockSpec((1, rows, width), lambda r, *_: (r, 0, 0)),
                pl.BlockSpec((1, 2, rows, HEAD_SIZE), lambda r, *_: (r, 0, 0, 0)),
                pl.BlockSpec(memory_space=pl.ANY),
            ],
            out_specs=pl.BlockSpec((1, rows, width), lambda r, *_: (r, 0, 0)),
            scratch_shapes=[
                pltpu.VMEM(key_value.shape, jnp.bfloat16),
                pltpu.SemaphoreType.DMA((2,)),
            ],
        ),
        compiler_params=pltpu.CompilerParams(vmem_limit_bytes=48 * 1024 * 1024),
        cost_estimate=pl.CostEstimate(
            flops=4 * 1024 * 1024 * 1024, bytes_accessed=24 * 1024 * 1024, transcendentals=0
        ),
    )(table, count, length, query, own, key_value)


def slot_lookup(cited_ids, lookup_table):
    matches = cited_ids[..., None] == jnp.arange(lookup_table.shape[0])
    return jnp.sum(jnp.where(matches, lookup_table, 0), axis=-1)


def block_table(slots, blocks):
    ends = jnp.cumsum(blocks, axis=1)
    begins = ends - blocks
    index = jnp.arange(MOST + 1)[None, None, :]
    inside = (index >= begins[..., None]) & (index < ends[..., None])
    number = slots[..., None] * PBLK + index - begins[..., None]
    return jnp.sum(jnp.where(inside, number, 0), axis=1), ends[:, -1]


def body(
    passage_query,
    passage_key_value,
    passage_length,
    passage_slot,
    cites,
    question_query,
    question_key_value,
    question_length,
):
    all_rows = lax.all_gather(passage_key_value, "work", axis=1, tiled=True)
    all_blocks = all_rows.reshape(2, -1, BLOCK, HEAD_SIZE)

    width = GROUP * HEAD_SIZE
    query = question_query.reshape(QUESTION_LENGTH, KEY_VALUE_HEADS, width)
    own = question_key_value.reshape(QUESTION_LENGTH, 2, KEY_VALUE_HEADS, HEAD_SIZE)
    query = lax.all_to_all(jnp.transpose(query, (1, 0, 2)), "req", 0, 0, tiled=True)
    own = lax.all_to_all(jnp.transpose(own, (2, 1, 0, 3)), "req", 0, 0, tiled=True)

    facts = jnp.concatenate([cites, question_length[:, None]], axis=1)
    facts = lax.all_gather(facts, "req", axis=0, tiled=True)
    slots = slot_lookup(facts[:, :CITED_PASSAGES], passage_slot)
    table, count = block_table(slots, slot_lookup(slots, passage_length))

    slot_total = passage_query.shape[0] // PASSAGE_ROWS
    my_blocks = lax.dynamic_slice_in_dim(
        passage_length, lax.axis_index("work") * slot_total, slot_total
    )
    passage_output = passage_attention(my_blocks, passage_query, passage_key_value)

    answer = question_attention(
        table.reshape(-1), count, facts[:, CITED_PASSAGES], query, own, all_blocks
    )
    answer = lax.all_to_all(answer, "req", 0, 0, tiled=True)
    question_output = jnp.transpose(answer, (1, 0, 2)).reshape(QUESTION_LENGTH, -1)
    return (passage_output, question_output)


def solution(mesh):
    return jax.shard_map(
        body,
        mesh=mesh,
        in_specs=(
            P("work", "req"),
            P(None, "work", "req"),
            P(),
            P(),
            P(("req", "work"), None),
            P(("req", "work"), None),
            P(("req", "work"), None, None),
            P(("req", "work")),
        ),
        out_specs=(P("work", "req"), P(("req", "work"), None)),
        check_vma=False,
    )
```

time: 410 us -> 233 us (0.57)
  the two profiles are of different devices: /device:TPU:1 before, /device:TPU:8 now
where the time goes in v1:
time: 233 us; the launch traced here: 231 us
  waiting for transfers between devices  121 us (52%)
  Pallas kernels  36.7 us (16%)
  blocking collectives  29.3 us (13%)
  local copies, waits for them, and re-layouts  15.9 us (7%)
  between operations  14.8 us (6%)
  starting transfers between devices  12.9 us (6%)
    all_gather x1, waiting for transfers between devices, body(): all_rows = lax.all_gather(passage_key_value, 'work', axis=1, tiled=True)  93.1 us
    pallas_call x1, Pallas kernels, question_attention(): pl.pallas_call(question_kernel, out_shape=jax.ShapeDtypeStruct(query.shap...  32.5 us
    all_gather x1, blocking collectives, body(): facts = lax.all_gather(facts, 'req', axis=0, tiled=True)  29.3 us
    all_to_all x1, waiting for transfers between devices, body(): answer = lax.all_to_all(answer, 'req', 0, 0, tiled=True)  22.7 us
    unnamed x15, local copies, waits for them, and re-layouts  8.82 us
    all_to_all x1, starting transfers between devices, body(): answer = lax.all_to_all(answer, 'req', 0, 0, tiled=True)  4.79 us
  transfers between devices with their start and end apart: 4, of which 3 were waited for; matrix products, arithmetic and copies ran while one was open for 4% of the time, Pallas kernels for 2%

profile of v1, /device:TPU:8, one launch (start us, length us, event | category | flops | bytes accessed | tf_op | source)
XLA Modules:
  0.0 231.2 jit_solution(17350013196589606689)
XLA Ops:
  7.2 0.0 all-gather.3.cloned.1.call-start
  7.2 0.7 all-gather.3.cloned.1.call-update
  7.9 1.4 copy.31
  9.3 1.0 copy.32
  10.3 4.3 %all-to-all-start.1 = ((bf16[8,2,128,128]{3,2,1,0:T(8,128)(2,1)}), bf16[8,2,128,128]{3,2,1,0:T(8,128)(2,1)S(1)}, u32[]{:S(2)}, u32[]{:S(2)}) async-start(bf16[8,2,128,128]{3,2,1,0:T(8,128)(2,1)} %bitcast.7), calls=%async_computation.1 | async-start | bytes 1048576 | tf_op jit(solution)/shard_map/all_to_all | solution.py:200
  14.6 3.2 %copy.29 = bf16[128,8192]{0,1:T(8,128)(2,1)S(1)} copy(bf16[128,8192]{1,0:T(8,128)(2,1)} %param.13) | data formatting | bytes 4194304 | tf_op args[5]
  17.8 2.6 %copy.30 = bf16[128,8,1024]{2,0,1:T(8,128)(2,1)} copy(bf16[128,8,1024]{0,2,1:T(8,128)(2,1)S(1)} %bitcast.18) | data formatting | bytes 4194304 | tf_op jit(solution)/shard_map/reshape | solution.py:197
  20.4 4.5 %all-to-all-done.1.own_ref = bf16[8,2,128,128]{3,2,1,0:T(8,128)(2,1)S(1)} async-done(((bf16[8,2,128,128]{3,2,1,0:T(8,128)(2,1)}), bf16[8,2,128,128]{3,2,1,0:T(8,128)(2,1)S(1)}, u32[]{:S(2)}, u32[]{:S(2)}) %all-to-all-start.1) | async-done | bytes 524320 | tf_op jit(solution)/shard_map/all_to_all | solution.py:200
  24.9 0.0 copy-start.5
  24.9 0.0 copy-start.3
  24.9 0.0 copy-start.4
  24.9 3.8 %all-to-all-start = ((bf16[8,128,1024]{2,1,0:T(8,128)(2,1)}), bf16[8,128,1024]{2,1,0:T(8,128)(2,1)S(1)}, u32[]{:S(2)}, u32[]{:S(2)}) async-start(bf16[8,128,1024]{2,1,0:T(8,128)(2,1)} %bitcast.16), calls=%async_computation | async-start | bytes 4194304 | tf_op jit(solution)/shard_map/all_to_all | solution.py:199
  29.4 0.0 copy-done.5
  29.4 0.1 add_bitcast_fusion
  29.5 29.3 %all-gather = s32[8,1,5]{2,1,0:T(1,128)S(1)} all-gather(s32[1,1,5]{2,1,0:T(1,128)S(1)} %add_bitcast_fusion), channel_id=1, replica_groups=mesh['req'=8,'work'=32] {'req'}, dimensions={0}, use_global_device_ids=true | all-gather | bytes 180 | tf_op jit(solution)/shard_map/all_gather | solution.py:203
  58.7 0.1 copy.28
  58.8 0.0 copy-done.3
  58.8 0.2 select_reduce_fusion.2
  59.0 0.0 copy-done.4
  59.0 0.2 select_reduce_fusion.1
  59.3 0.1 select_reduce_fusion
  59.4 0.1 reshape.31.table_ref
  59.5 0.2 slice_reduce_fusion.length_ref
  59.7 0.0 all-to-all-done.q_ref
  59.7 93.1 %all-gather.3.cloned.1.call-done = bf16[2,32768,128]{2,1,0:T(8,128)(2,1)} async-done(((bf16[2,1024,128]{2,1,0:T(8,128)(2,1)}), bf16[2,32768,128]{2,1,0:T(8,128)(2,1)}) %all-gather.3.cloned.1.call-update) | async-done | bytes 16777232 | tf_op jit(solution)/shard_map/all_gather | solution.py:193
  152.8 32.5 %shard_map.96 = bf16[8,128,1024]{2,1,0:T(8,128)(2,1)S(1)} custom-call(s32[136]{0:T(256)S(1)} %reshape.31.table_ref, s32[8]{0:T(128)S(1)} %slice_bitcast_fusion.count_ref, s32[8]{0:T(128)S(1)} %slice_reduce_fusion.length_ref, bf16[8,128,1024]{2,1,0:T(8,128)(2,1)S(1)} %all-to-all-done.q_ref, bf16[8,2,128,128]{3,2,1,0:T(8,128)(2,1)S(1)} %all-to-all-done.1.own_ref, ...), custom_call_target="tpu_custom_call" | custom-call | flops 4294967296 | bytes 25165824 | tf_op jit(solution)/shard_map/pallas_call | solution.py:145
  185.3 0.0 copy-start
  185.3 1.3 copy-done
  186.6 0.0 copy-start.1
  186.6 0.0 copy-start.2
  186.6 4.8 %all-to-all-start.2 = ((bf16[8,128,1024]{2,1,0:T(8,128)(2,1)}), bf16[8,128,1024]{2,1,0:T(8,128)(2,1)}, u32[]{:S(2)}, u32[]{:S(2)}) async-start(bf16[8,128,1024]{2,1,0:T(8,128)(2,1)} %copy-done), calls=%async_computation.2 | async-start | bytes 4194304 | tf_op jit(solution)/shard_map/all_to_all | solution.py:216
  191.4 0.1 dynamic_slice.3.blocks_ref
  191.5 0.0 copy-done.1
  191.5 0.0 copy-done.2
  191.5 4.3 %shard_map.95 = bf16[1024,1024]{1,0:T(8,128)(2,1)} custom-call(s32[2]{0:T(128)S(1)} %dynamic_slice.3.blocks_ref, bf16[1024,1024]{1,0:T(8,128)(2,1)S(1)} %copy-done.2, bf16[2,1024,128]{2,1,0:T(8,128)(2,1)S(1)} %copy-done.1), custom_call_target="tpu_custom_call" | custom-call | flops 2147483648 | bytes 5242880 | tf_op jit(solution)/shard_map/pallas_call | solution.py:69
  195.7 22.7 %all-to-all-done.2 = bf16[8,128,1024]{2,1,0:T(8,128)(2,1)} async-done(((bf16[8,128,1024]{2,1,0:T(8,128)(2,1)}), bf16[8,128,1024]{2,1,0:T(8,128)(2,1)}, u32[]{:S(2)}, u32[]{:S(2)}) %all-to-all-start.2) | async-done | bytes 2097184 | tf_op jit(solution)/shard_map/all_to_all | solution.py:216
  218.4 3.0 %copy.33 = bf16[128,8,1024]{0,2,1:T(8,128)(2,1)S(1)} copy(bf16[128,8,1024]{2,0,1:T(8,128)(2,1)} %bitcast.9) | data formatting | bytes 4194304 | tf_op jit(solution)/shard_map/transpose | solution.py:217
  221.4 2.9 %copy.34 = bf16[128,8192]{1,0:T(8,128)(2,1)} copy(bf16[128,8192]{0,1:T(8,128)(2,1)S(1)} %bitcast.17) | data formatting | bytes 4194304
  (4 shorter events, 0.1 us)
Async XLA Ops:
  7.2 145.6 %all-gather.3.cloned.1.call-start = ((), (), s32[]{:S(2)}) async-start(), calls=%async_computation.3 | async-start | bytes 17301504 | tf_op jit(solution)/shard_map/all_gather | solution.py:193
  10.3 14.6 %all-to-all-start.1 = ((bf16[8,2,128,128]{3,2,1,0:T(8,128)(2,1)}), bf16[8,2,128,128]{3,2,1,0:T(8,128)(2,1)S(1)}, u32[]{:S(2)}, u32[]{:S(2)}) async-start(bf16[8,2,128,128]{3,2,1,0:T(8,128)(2,1)} %bitcast.7), calls=%async_computation.1 | async-start | bytes 1048576 | tf_op jit(solution)/shard_map/all_to_all | solution.py:200
  24.9 4.4 %copy-start.5 = (s32[1,4]{1,0:T(1,128)S(1)}, s32[1,4]{1,0:T(1,128)}, u32[]{:S(2)}) copy-start(s32[1,4]{1,0:T(1,128)} %param.12) | copy-start | bytes 52
  24.9 33.9 %copy-start.3 = (s32[64]{0:T(128)S(1)}, s32[64]{0:T(128)}, u32[]{:S(2)}) copy-start(s32[64]{0:T(128)} %param.11) | copy-start | bytes 772
  24.9 34.1 %copy-start.4 = (s32[64]{0:T(128)S(1)}, s32[64]{0:T(128)}, u32[]{:S(2)}) copy-start(s32[64]{0:T(128)} %param.10) | copy-start | bytes 772
  24.9 34.7 %all-to-all-start = ((bf16[8,128,1024]{2,1,0:T(8,128)(2,1)}), bf16[8,128,1024]{2,1,0:T(8,128)(2,1)S(1)}, u32[]{:S(2)}, u32[]{:S(2)}) async-start(bf16[8,128,1024]{2,1,0:T(8,128)(2,1)} %bitcast.16), calls=%async_computation | async-start | bytes 4194304 | tf_op jit(solution)/shard_map/all_to_all | solution.py:199
  185.3 1.3 copy-start
  186.6 4.9 %copy-start.1 = (bf16[2,1024,128]{2,1,0:T(8,128)(2,1)S(1)}, bf16[2,1024,128]{2,1,0:T(8,128)(2,1)}, u32[]{:S(2)}) copy-start(bf16[2,1024,128]{2,1,0:T(8,128)(2,1)} %kv_ref.1) | copy-start | bytes 1572868
  186.6 4.9 %copy-start.2 = (bf16[1024,1024]{1,0:T(8,128)(2,1)S(1)}, bf16[1024,1024]{1,0:T(8,128)(2,1)}, u32[]{:S(2)}) copy-start(bf16[1024,1024]{1,0:T(8,128)(2,1)} %q_ref.1) | copy-start | bytes 6291460
  186.6 31.8 %all-to-all-start.2 = ((bf16[8,128,1024]{2,1,0:T(8,128)(2,1)}), bf16[8,128,1024]{2,1,0:T(8,128)(2,1)}, u32[]{:S(2)}, u32[]{:S(2)}) async-start(bf16[8,128,1024]{2,1,0:T(8,128)(2,1)} %copy-done), calls=%async_computation.2 | async-start | bytes 4194304 | tf_op jit(solution)/shard_map/all_to_all | solution.py:216
Sparse Core Ops, SparseCore 0:
  10.6 142.1 all-gather.2

commit v2 on v1

v2 whole, which is shorter than its diff:
```python
import math

import jax
import jax.numpy as jnp
from jax import lax
from jax.experimental import pallas as pl
from jax.experimental.pallas import tpu as pltpu
from jax.sharding import PartitionSpec as P

QUERY_HEADS = 64
KEY_VALUE_HEADS = 8
GROUP = QUERY_HEADS // KEY_VALUE_HEADS
HEAD_SIZE = 128
BLOCK = 128
PBLK = 4
CITED_PASSAGES = 4
QUESTION_LENGTH = 128
PASSAGE_ROWS = 512
SCALE = math.log2(math.e) / math.sqrt(HEAD_SIZE)
LOW = -1e30
TILE = 64
LOTS = 2
MOST = CITED_PASSAGES * PBLK
WORK_Z, WORK_Y = 8, 4
SLOTS = 2
KEPT = 6
EXTRA = SLOTS * PBLK - KEPT
FIRST = 6
SECOND = WORK_Z * EXTRA - FIRST
GATHERED = WORK_Z * WORK_Y * KEPT
Z_ORDER = (0, 1, 3, 5, 7, 6, 4, 2)
Y_ORDER = (0, 1, 3, 2)
OWN_ROW = GROUP * QUESTION_LENGTH
FACT_ROW = OWN_ROW + 2 * QUESTION_LENGTH
PAYLOAD = FACT_ROW + 16
DOT_NT = (((1,), (1,)), ((), ()))


def stack_heads(ref_rows):
    return jnp.concatenate(
        [ref_rows[:, h * HEAD_SIZE : (h + 1) * HEAD_SIZE] for h in range(GROUP)], axis=0
    )


def with_ones(values):
    return jnp.concatenate([values, jnp.ones_like(values)], axis=1)


def passage_kernel(blocks_ref, q_ref, kv_ref, out_ref):
    slot = pl.program_id(0)
    blocks = blocks_ref[slot]
    rows = GROUP * BLOCK
    row = lax.broadcasted_iota(jnp.int32, (rows, BLOCK), 0) % BLOCK
    column = lax.broadcasted_iota(jnp.int32, (rows, BLOCK), 1)
    causal = column <= row
    for i in range(PBLK):
        place = slice(i * BLOCK, (i + 1) * BLOCK)

        @pl.when(i < blocks)
        def _():
            q = stack_heads(q_ref[place, :])
            k = kv_ref[0, : (i + 1) * BLOCK, :]
            v = with_ones(kv_ref[1, : (i + 1) * BLOCK, :])
            s = lax.dot_general(q, k, DOT_NT, preferred_element_type=jnp.float32)
            last = jnp.where(causal, s[:, i * BLOCK :], LOW)
            s = last if i == 0 else jnp.concatenate([s[:, : i * BLOCK], last], axis=1)
            m = jnp.max(s, axis=1, keepdims=True)
            p = jnp.exp2((s - m) * SCALE).astype(jnp.bfloat16)
            o = jnp.dot(p, v, preferred_element_type=jnp.float32)
            o = (o[:, :HEAD_SIZE] / o[:, HEAD_SIZE:]).astype(jnp.bfloat16)
            for h in range(GROUP):
                out_ref[place, h * HEAD_SIZE : (h + 1) * HEAD_SIZE] = o[h * BLOCK : (h + 1) * BLOCK]

        @pl.when(i >= blocks)
        def _():
            out_ref[place, :] = jnp.zeros((BLOCK, GROUP * HEAD_SIZE), jnp.bfloat16)


def passage_attention(blocks, query, key_value):
    slots = query.shape[0] // PASSAGE_ROWS
    width = GROUP * HEAD_SIZE
    return pl.pallas_call(
        passage_kernel,
        out_shape=jax.ShapeDtypeStruct(query.shape, jnp.bfloat16),
        grid_spec=pltpu.PrefetchScalarGridSpec(
            num_scalar_prefetch=1,
            grid=(slots,),
            in_specs=[
                pl.BlockSpec((PASSAGE_ROWS, width), lambda s, b: (s, 0)),
                pl.BlockSpec((2, PASSAGE_ROWS, HEAD_SIZE), lambda s, b: (0, s, 0)),
            ],
            out_specs=pl.BlockSpec((PASSAGE_ROWS, width), lambda s, b: (s, 0)),
        ),
        compiler_params=pltpu.CompilerParams(vmem_limit_bytes=40 * 1024 * 1024),
        cost_estimate=pl.CostEstimate(
            flops=slots * 4 * 1024 * 512 * 512, bytes_accessed=5 * 1024 * 1024, transcendentals=0
        ),
    )(blocks, query, key_value)


def bundle_kernel(q_ref, k_ref, v_ref, facts_ref, out_ref):
    for h in range(GROUP):
        out_ref[0, h * QUESTION_LENGTH : (h + 1) * QUESTION_LENGTH, :] = q_ref[
            :, h * HEAD_SIZE : (h + 1) * HEAD_SIZE
        ]
    out_ref[0, OWN_ROW : OWN_ROW + QUESTION_LENGTH, :] = k_ref[...].T
    out_ref[0, OWN_ROW + QUESTION_LENGTH : FACT_ROW, :] = v_ref[...]
    out_ref[0, FACT_ROW:, :] = facts_ref[...]


def bundle(query, own, facts):
    width = GROUP * HEAD_SIZE
    return pl.pallas_call(
        bundle_kernel,
        out_shape=jax.ShapeDtypeStruct((KEY_VALUE_HEADS, PAYLOAD, HEAD_SIZE), jnp.bfloat16),
        grid=(KEY_VALUE_HEADS,),
        in_specs=[
            pl.BlockSpec((QUESTION_LENGTH, width), lambda g: (0, g)),
            pl.BlockSpec((QUESTION_LENGTH, HEAD_SIZE), lambda g: (0, g)),
            pl.BlockSpec((QUESTION_LENGTH, HEAD_SIZE), lambda g: (0, KEY_VALUE_HEADS + g)),
            pl.BlockSpec((16, HEAD_SIZE), lambda g: (0, 0)),
        ],
        out_specs=pl.BlockSpec((1, PAYLOAD, HEAD_SIZE), lambda g: (g, 0, 0)),
        cost_estimate=pl.CostEstimate(flops=0, bytes_accessed=5 * 1024 * 1024, transcendentals=0),
    )(query, own, own, facts)


def spread_kernel(in_ref, out_ref):
    for g in range(in_ref.shape[0]):
        for h in range(GROUP):
            first = (g * GROUP + h) * HEAD_SIZE
            out_ref[:, first : first + HEAD_SIZE] = in_ref[
                g, h * QUESTION_LENGTH : (h + 1) * QUESTION_LENGTH, :
            ]


def spread(answer):
    groups = 2
    width = groups * GROUP * HEAD_SIZE
    return pl.pallas_call(
        spread_kernel,
        out_shape=jax.ShapeDtypeStruct((QUESTION_LENGTH, QUERY_HEADS * HEAD_SIZE), jnp.bfloat16),
        grid=(KEY_VALUE_HEADS // groups,),
        in_specs=[pl.BlockSpec((groups, OWN_ROW, HEAD_SIZE), lambda g: (g, 0, 0))],
        out_specs=pl.BlockSpec((QUESTION_LENGTH, width), lambda g: (0, g)),
        cost_estimate=pl.CostEstimate(flops=0, bytes_accessed=4 * 1024 * 1024, transcendentals=0),
    )(answer)


def order_kernel(length_ref, kv_ref, kept_ref, *refs):
    worker = lax.axis_index("work")
    before = 0
    for slot in range(SLOTS):
        length = length_ref[worker * SLOTS + slot]
        for block in range(PBLK):
            rows = slice((slot * PBLK + block) * BLOCK, (slot * PBLK + block + 1) * BLOCK)

            def put(ref, place):
                ref[place, 0] = kv_ref[0, rows, :].T
                ref[place, 1] = kv_ref[1, rows, :]

            place = before + block
            pl.when((block < length) & (place < KEPT))(lambda place=place: put(kept_ref, place))
            if refs:
                pl.when((block < length) & (place >= KEPT))(
                    lambda place=place: put(refs[0], place - KEPT)
                )
        before = before + length


def order(passage_length, key_value):
    shapes = [
        jax.ShapeDtypeStruct((size, 2, BLOCK, HEAD_SIZE), jnp.bfloat16)
        for size in (KEPT, EXTRA)
        if size
    ]
    return pl.pallas_call(
        order_kernel,
        out_shape=shapes,
        in_specs=[pl.BlockSpec(memory_space=pltpu.SMEM), pl.BlockSpec(memory_space=pltpu.VMEM)],
        out_specs=[pl.BlockSpec(memory_space=pltpu.VMEM)] * len(shapes),
        cost_estimate=pl.CostEstimate(flops=0, bytes_accessed=1024 * 1024, transcendentals=0),
    )(passage_length, key_value)


def pack_kernel(place_ref, *refs):
    sources, outs = refs[:-2], refs[-2:]
    blocks = [(source, i) for source in sources for i in range(source.shape[0])]
    for index, (source, i) in enumerate(blocks):
        place = place_ref[index]

        @pl.when((place >= 0) & (place < FIRST))
        def _():
            outs[0][place] = source[i]

        @pl.when(place >= FIRST)
        def _():
            outs[1][place - FIRST] = source[i]


def pack(place, sources):
    return pl.pallas_call(
        pack_kernel,
        out_shape=[
            jax.ShapeDtypeStruct((size, *sources[0].shape[1:]), jnp.bfloat16)
            for size in (FIRST, SECOND)
        ],
        in_specs=[pl.BlockSpec(memory_space=pltpu.SMEM)]
        + [pl.BlockSpec(memory_space=pltpu.VMEM)] * len(sources),
        out_specs=[pl.BlockSpec(memory_space=pltpu.VMEM)] * 2,
        cost_estimate=pl.CostEstimate(flops=0, bytes_accessed=2 * 1024 * 1024, transcendentals=0),
    )(place, *sources)


def question_kernel(table_ref, count_ref, length_ref, in_ref, *refs):
    pieces, out_ref, store, sems = refs[:-3], refs[-3], refs[-2], refs[-1]
    request = pl.program_id(0)
    total = pl.num_programs(0)

    def start(which, carry):
        def one(index, carry):
            place = table_ref[which * (MOST + 1) + index]
            low = 0
            for piece in pieces:
                size = piece.shape[0]

                @pl.when((place >= low) & (place < low + size))
                def _():
                    pltpu.make_async_copy(
                        piece.at[place - low], store.at[which, index], sems.at[which, index]
                    ).start()

                low += size
            return carry

        return lax.fori_loop(0, count_ref[which], one, carry)

    @pl.when(request == 0)
    def _():
        lax.fori_loop(0, total, start, 0)

    length = length_ref[request]
    count = count_ref[request]

    def wait(index, carry):
        pltpu.make_async_copy(
            pieces[0].at[0], store.at[request, index], sems.at[request, index]
        ).wait()
        return carry

    lax.fori_loop(0, count, wait, 0)
    rows = GROUP // LOTS * TILE
    row = lax.broadcasted_iota(jnp.int32, (rows, BLOCK), 0) % TILE
    column = lax.broadcasted_iota(jnp.int32, (rows, BLOCK), 1)

    def attend(cited):
        @pl.when(count < cited)
        def _():
            store[request, cited - 1] = jnp.zeros(store.shape[2:], store.dtype)

        extra = jnp.where(count < cited, LOW, 0.0)

        def tile_step(tile, carry):
            first = pl.multiple_of(tile * TILE, TILE)
            k = [in_ref[0, OWN_ROW : OWN_ROW + BLOCK, :]] + [store[request, i, 0] for i in range(cited)]
            v = [in_ref[0, OWN_ROW + BLOCK : FACT_ROW, :]] + [store[request, i, 1] for i in range(cited)]
            k = jnp.concatenate(k, axis=1)
            v = with_ones(jnp.concatenate(v, axis=0))
            lot = GROUP // LOTS

            def score(heads):
                q = jnp.concatenate(
                    [in_ref[0, pl.ds(h * QUESTION_LENGTH + first, TILE), :] for h in heads], axis=0
                )
                s = jnp.dot(q, k, preferred_element_type=jnp.float32)
                return jnp.concatenate(
                    [
                        jnp.where(column <= row + first, s[:, :BLOCK], LOW),
                        s[:, BLOCK:-BLOCK],
                        s[:, -BLOCK:] + extra,
                    ],
                    axis=1,
                )

            def finish(heads, s):
                m = jnp.max(s, axis=1, keepdims=True)
                p = jnp.exp2((s - m) * SCALE).astype(jnp.bfloat16)
                o = jnp.dot(p, v, preferred_element_type=jnp.float32)
                o = o[:, :HEAD_SIZE] / o[:, HEAD_SIZE:]
                o = jnp.where(row + first < length, o, 0.0).astype(jnp.bfloat16)
                for i, h in enumerate(heads):
                    out_ref[0, pl.ds(h * QUESTION_LENGTH + first, TILE), :] = o[
                        i * TILE : (i + 1) * TILE
                    ]

            lots = [range(i * lot, (i + 1) * lot) for i in range(LOTS)]
            s = score(lots[0])
            for i in range(LOTS):
                following = score(lots[i + 1]) if i + 1 < LOTS else None
                finish(lots[i], s)
                s = following
            return carry

        lax.fori_loop(0, (length + TILE - 1) // TILE, tile_step, 0)

    def clear(tile, carry):
        for h in range(GROUP):
            out_ref[0, pl.ds(h * QUESTION_LENGTH + pl.multiple_of(tile * TILE, TILE), TILE), :] = (
                jnp.zeros((TILE, HEAD_SIZE), out_ref.dtype)
            )
        return carry

    lax.fori_loop((length + TILE - 1) // TILE, QUESTION_LENGTH // TILE, clear, 0)

    for cited in range(CITED_PASSAGES + 1, MOST + 2, 2):
        pl.when(count // 2 * 2 + 1 == cited)(lambda cited=cited: attend(cited))


def question_attention(table, count, length, payload, pieces):
    requests = payload.shape[0]
    return pl.pallas_call(
        question_kernel,
        out_shape=jax.ShapeDtypeStruct((requests, OWN_ROW, HEAD_SIZE), jnp.bfloat16),
        grid_spec=pltpu.PrefetchScalarGridSpec(
            num_scalar_prefetch=3,
            grid=(requests,),
            in_specs=[pl.BlockSpec((1, PAYLOAD, HEAD_SIZE), lambda r, *_: (r, 0, 0))]
            + [pl.BlockSpec(memory_space=pl.ANY)] * len(pieces),
            out_specs=pl.BlockSpec((1, OWN_ROW, HEAD_SIZE), lambda r, *_: (r, 0, 0)),
            scratch_shapes=[
                pltpu.VMEM((requests, MOST + 1, *pieces[0].shape[1:]), jnp.bfloat16),
                pltpu.SemaphoreType.DMA((requests, MOST)),
            ],
        ),
        compiler_params=pltpu.CompilerParams(vmem_limit_bytes=40 * 1024 * 1024),
        cost_estimate=pl.CostEstimate(
            flops=4 * 1024 * 1024 * 1024, bytes_accessed=24 * 1024 * 1024, transcendentals=0
        ),
    )(table, count, length, payload, *pieces)


def step_z(array, by):
    steps = [
        (z * WORK_Y + y, (z + by) % WORK_Z * WORK_Y + y) for z in range(WORK_Z) for y in range(WORK_Y)
    ]
    return lax.ppermute(array, "work", steps)


def step_y(array, by):
    steps = [
        (z * WORK_Y + y, z * WORK_Y + (y + by) % WORK_Y) for z in range(WORK_Z) for y in range(WORK_Y)
    ]
    return lax.ppermute(array, "work", steps)


def ring_z(chunk):
    out = [chunk]
    up = down = chunk
    for _ in range(WORK_Z // 2 - 1):
        up, down = step_z(up, 1), step_z(down, -1)
        out += [up, down]
    half = chunk.shape[0] // 2
    return out + [step_z(up[:half], 1), step_z(down[half:], -1)]


def ring_y(chunk):
    half = chunk.shape[0] // 2
    up, down = step_y(chunk, 1), step_y(chunk, -1)
    return [chunk, up, down, step_y(up[:half], 1), step_y(down[half:], -1)]


def pick(index, values):
    values = jnp.asarray(values, jnp.int32)
    return jnp.sum(
        jnp.where(index[..., None] == jnp.arange(values.shape[0]), values, 0), axis=-1
    )


def block_places(passage_length, y):
    lengths = passage_length.reshape(WORK_Z, WORK_Y, SLOTS)
    ahead = jnp.concatenate([jnp.zeros_like(lengths[..., :1]), lengths[..., :1]], axis=-1)
    at = ahead[..., None] + jnp.arange(PBLK)
    worker = jnp.arange(WORK_Z)[:, None] * WORK_Y + jnp.arange(WORK_Y)
    gathered = worker[..., None, None] * KEPT + at
    if not EXTRA:
        return gathered.reshape(-1, PBLK), None, None
    beyond = jnp.maximum(jnp.sum(lengths, axis=-1) - KEPT, 0)
    earlier = jnp.arange(WORK_Z)
    earlier = (earlier[:, None] < earlier[None, :]).astype(jnp.int32)
    begins = jnp.sum(earlier[:, :, None] * beyond[:, None, :], axis=0)
    index = jnp.arange(EXTRA)
    lists = jnp.where(index < beyond[..., None], begins[..., None] + index, -1)
    place = begins[..., None, None] + at - KEPT
    y_place = pick((y - jnp.arange(WORK_Y)) % WORK_Y, Y_ORDER)[None, :, None, None]
    place = jnp.where(
        place < FIRST,
        GATHERED + y_place * FIRST + place,
        GATHERED + WORK_Y * FIRST + y_place * SECOND + place - FIRST,
    )
    places = jnp.where(at < KEPT, gathered, place)
    return places.reshape(-1, PBLK), lists, jnp.sum(beyond, axis=0)


def block_table(cited, passage_slot, passage_length, places):
    slots = pick(cited, passage_slot)
    hit = slots[..., None] == jnp.arange(passage_length.shape[0])
    blocks = jnp.sum(jnp.where(hit, passage_length, 0), axis=-1)
    found = jnp.sum(jnp.where(hit[..., None], places, 0), axis=2)
    earlier = jnp.arange(CITED_PASSAGES)
    earlier = earlier[:, None] < earlier[None, :]
    begins = jnp.sum(jnp.where(earlier, blocks[:, :, None], 0), axis=1)
    block = jnp.arange(PBLK)
    order = jnp.where(block < blocks[..., None], begins[..., None] + block, -1)
    mine = order[..., None] == jnp.arange(MOST + 1)
    table = jnp.sum(jnp.where(mine, found[..., None], 0), axis=(1, 2))
    return table.reshape(-1), jnp.sum(blocks, axis=1)


def body(
    passage_query,
    passage_key_value,
    passage_length,
    passage_slot,
    cites,
    question_query,
    question_key_value,
    question_length,
):
    worker = lax.axis_index("work")
    z, y = worker // WORK_Y, worker % WORK_Y
    kept, *beyond = order(passage_length, passage_key_value)
    pieces = [lax.all_gather(kept, "work", axis=0, tiled=True)]
    places, lists, live = block_places(passage_length, y)

    facts = jnp.concatenate([cites, question_length[:, None]], axis=1).astype(jnp.bfloat16)
    facts = jnp.pad(facts, ((0, 15), (0, HEAD_SIZE - CITED_PASSAGES - 1)))
    payload = bundle(question_query, question_key_value.reshape(QUESTION_LENGTH, -1), facts)
    payload = lax.all_to_all(payload, "req", 0, 0, tiled=True)

    if EXTRA:
        beyond = ring_z(beyond[0])
        z_from = (z - jnp.asarray([Z_ORDER.index(i) for i in range(WORK_Z)])) % WORK_Z
        mine = jnp.sum(jnp.where(jnp.arange(WORK_Y)[:, None] == y, lists, 0), axis=1)
        hit = z_from[:, None] == jnp.arange(WORK_Z)
        mine = jnp.sum(jnp.where(hit[..., None], mine[None], 0), axis=1)
        first, second = pack(mine.reshape(-1), beyond)
        pieces.append(jnp.concatenate(ring_y(first), axis=0))
        pieces.append(
            lax.cond(
                jnp.max(live) > FIRST,
                lambda part: jnp.concatenate(ring_y(part), axis=0),
                lambda part: jnp.zeros((WORK_Y * SECOND, *part.shape[1:]), part.dtype),
                second,
            )
        )

    slot_total = passage_query.shape[0] // PASSAGE_ROWS
    my_blocks = lax.dynamic_slice_in_dim(passage_length, worker * slot_total, slot_total)
    passage_output = passage_attention(my_blocks, passage_query, passage_key_value)

    facts = payload[:, FACT_ROW, : CITED_PASSAGES + 1].astype(jnp.int32)
    table, count = block_table(facts[:, :CITED_PASSAGES], passage_slot, passage_length, places)
    answer = question_attention(table, count, facts[:, CITED_PASSAGES], payload, pieces)
    answer = lax.all_to_all(answer, "req", 0, 0, tiled=True)
    return passage_output, spread(answer)


def solution(mesh):
    return jax.shard_map(
        body,
        mesh=mesh,
        in_specs=(
            P("work", "req"),
            P(None, "work", "req"),
            P(),
            P(),
            P(("req", "work"), None),
            P(("req", "work"), None),
            P(("req", "work"), None, None),
            P(("req", "work")),
        ),
        out_specs=(P("work", "req"), P(("req", "work"), None)),
        check_vma=False,
    )
```

time: 233 us -> 207 us (0.89)
  the two profiles are of different devices: /device:TPU:8 before, /device:TPU:1 now
where the time goes in v2:
time: 207 us; the launch traced here: 204 us
  waiting for transfers between devices  100 us (48%)
  Pallas kernels  37.7 us (18%)
  starting transfers between devices  33.1 us (16%)
  between operations  15.7 us (8%)
  local copies, waits for them, and re-layouts  13 us (6%)
  other arithmetic  4.66 us (2%)
    all_gather x1, waiting for transfers between devices, body(): pieces = [lax.all_gather(kept, 'work', axis=0, tiled=True)]  55.7 us
    all_to_all x1, waiting for transfers between devices, body(): answer = lax.all_to_all(answer, 'req', 0, 0, tiled=True)  21.8 us
    pallas_call x1, Pallas kernels, question_attention(): pl.pallas_call(question_kernel, out_shape=jax.ShapeDtypeStruct((requests,...  18.4 us
    ppermute x8, starting transfers between devices, step_z(): return lax.ppermute(array, 'work', steps)  15 us
    ppermute x8, waiting for transfers between devices, step_z(): return lax.ppermute(array, 'work', steps)  11.9 us
    ppermute x4, waiting for transfers between devices, step_y(): return lax.ppermute(array, 'work', steps)  10.8 us
    ppermute x4, starting transfers between devices, step_y(): return lax.ppermute(array, 'work', steps)  7.1 us
    unnamed x35, local copies, waits for them, and re-layouts  7.03 us
  transfers between devices with their start and end apart: 15, of which 8 were waited for; matrix products, arithmetic and copies ran while one was open for 7% of the time, Pallas kernels for 6%

profile of v2, /device:TPU:1, one launch (start us, length us, event | category | flops | bytes accessed | tf_op | source)
XLA Modules:
  0.0 204.2 jit_solution(16574392537269637040)
XLA Ops:
  7.2 2.2 %shard_map.115 = (bf16[6,2,128,128]{3,2,1,0:T(8,128)(2,1)}, bf16[2,2,128,128]{3,2,1,0:T(8,128)(2,1)}) custom-call(s32[64]{0:T(128)} %length_ref.1, bf16[2,1024,128]{2,1,0:T(8,128)(2,1)} %kv_ref.3), custom_call_target="tpu_custom_call" | custom-call | bytes 1048576 | tf_op jit(solution)/shard_map/pallas_call | solution.py:177
  9.4 2.7 %collective-permute-start.4 = (bf16[2,2,128,128]{3,2,1,0:T(8,128)(2,1)}, bf16[2,2,128,128]{3,2,1,0:T(8,128)(2,1)S(1)}, u32[]{:S(2)}, u32[]{:S(2)}) collective-permute-start(bf16[2,2,128,128]{3,2,1,0:T(8,128)(2,1)} %get-tuple-element.11.refs_0_), channel_id=1, source_target_pairs={{0,4},{1,5},{2,6},{3,7},{4,8},{5,9},{6,10},{7,11},{8,12},{9,13},{1... | collective-permute-start | bytes 393224 | tf_op jit(solution)/shard_map/ppermute | solution.py:346
  12.1 4.2 %collective-permute-start.5 = (bf16[2,2,128,128]{3,2,1,0:T(8,128)(2,1)}, bf16[2,2,128,128]{3,2,1,0:T(8,128)(2,1)S(1)}, u32[]{:S(2)}, u32[]{:S(2)}) collective-permute-start(bf16[2,2,128,128]{3,2,1,0:T(8,128)(2,1)} %get-tuple-element.11.refs_0_), channel_id=1, source_target_pairs={{0,28},{1,29},{2,30},{3,31},{4,0},{5,1},{6,2},{7,3},{8,4},{9,5},{1... | collective-permute-start | bytes 393224 | tf_op jit(solution)/shard_map/ppermute | solution.py:346
  16.2 2.0 copy.21
  18.8 0.7 convert.8
  19.5 0.7 fusion.5.facts_ref
  20.2 6.1 %shard_map.114 = bf16[8,1296,128]{2,1,0:T(8,128)(2,1)} custom-call(bf16[128,8192]{1,0:T(8,128)(2,1)} %q_ref.3, bf16[128,2048]{1,0:T(8,128)(2,1)} %bitcast.6, bf16[128,2048]{1,0:T(8,128)(2,1)} %bitcast.7, bf16[16,128]{1,0:T(8,128)(2,1)} %fusion.5.facts_ref), custom_call_target="tpu_custom_call" | custom-call | bytes 5242880 | tf_op jit(solution)/shard_map/pallas_call | solution.py:113
  26.3 5.4 %all-to-all-start = ((bf16[8,1296,128]{2,1,0:T(8,128)(2,1)}), bf16[8,1296,128]{2,1,0:T(8,128)(2,1)S(1)}, u32[]{:S(2)}, u32[]{:S(2)}) async-start(bf16[8,1296,128]{2,1,0:T(8,128)(2,1)} %shard_map.114), calls=%async_computation | async-start | bytes 5308416 | tf_op jit(solution)/shard_map/all_to_all | solution.py:438
  31.7 0.1 reshape.178
  31.8 0.2 reduce_sum.111
  32.1 0.1 copy.17
  32.2 0.1 multiply_reduce_fusion
  32.4 0.1 copy.18
  32.5 0.1 select_reduce_fusion.4
  32.6 0.1 collective-permute-start.6
  32.7 2.6 %collective-permute-start.7 = (bf16[2,2,128,128]{3,2,1,0:T(8,128)(2,1)S(1)}, bf16[2,2,128,128]{3,2,1,0:T(8,128)(2,1)S(1)}, u32[]{:S(2)}, u32[]{:S(2)}) collective-permute-start(bf16[2,2,128,128]{3,2,1,0:T(8,128)(2,1)S(1)} %collective-permute-done.5.refs_2_), channel_id=1, source_target_pairs={{0,28},{1,29},{2,30},{3,31},{4,0},{5,1},{6,2},{7,3},{8,4},{9,5},{1... | collective-permute-start | bytes 393224 | tf_op jit(solution)/shard_map/ppermute | solution.py:346
  35.4 0.1 copy.19
  35.5 0.2 select_reduce_fusion.8
  35.7 5.4 %collective-permute-done.6.refs_3_ = bf16[2,2,128,128]{3,2,1,0:T(8,128)(2,1)S(1)} collective-permute-done((bf16[2,2,128,128]{3,2,1,0:T(8,128)(2,1)S(1)}, bf16[2,2,128,128]{3,2,1,0:T(8,128)(2,1)S(1)}, u32[]{:S(2)}, u32[]{:S(2)}) %collective-permute-start.6) | collective-permute-done | bytes 131104 | tf_op jit(solution)/shard_map/ppermute | solution.py:346
  41.1 2.7 %collective-permute-start.9 = (bf16[2,2,128,128]{3,2,1,0:T(8,128)(2,1)S(1)}, bf16[2,2,128,128]{3,2,1,0:T(8,128)(2,1)S(1)}, u32[]{:S(2)}, u32[]{:S(2)}) collective-permute-start(bf16[2,2,128,128]{3,2,1,0:T(8,128)(2,1)S(1)} %collective-permute-done.7.refs_4_), channel_id=1, source_target_pairs={{0,28},{1,29},{2,30},{3,31},{4,0},{5,1},{6,2},{7,3},{8,4},{9,5},{1... | collective-permute-start | bytes 393224 | tf_op jit(solution)/shard_map/ppermute | solution.py:346
  43.8 0.6 multiply_add_fusion.1
  44.4 5.2 %collective-permute-done.8.refs_5_ = bf16[2,2,128,128]{3,2,1,0:T(8,128)(2,1)S(1)} collective-permute-done((bf16[2,2,128,128]{3,2,1,0:T(8,128)(2,1)S(1)}, bf16[2,2,128,128]{3,2,1,0:T(8,128)(2,1)S(1)}, u32[]{:S(2)}, u32[]{:S(2)}) %collective-permute-start.8) | collective-permute-done | bytes 131104 | tf_op jit(solution)/shard_map/ppermute | solution.py:346
  49.6 0.1 collective-permute-start.10
  49.7 0.7 slice.43
  50.3 2.7 %collective-permute-start.11 = (bf16[1,2,128,128]{3,2,1,0:T(8,128)(2,1)}, bf16[1,2,128,128]{3,2,1,0:T(8,128)(2,1)}, u32[]{:S(2)}, u32[]{:S(2)}) collective-permute-start(bf16[1,2,128,128]{3,2,1,0:T(8,128)(2,1)} %slice.43), channel_id=1, source_target_pairs={{0,28},{1,29},{2,30},{3,31},{4,0},{5,1},{6,2},{7,3},{8,4},{9,5},{1... | collective-permute-start | bytes 196616 | tf_op jit(solution)/shard_map/ppermute | solution.py:346
  53.0 0.1 select_reduce_fusion.6
  53.2 0.1 copy.20
  53.2 0.6 reshape.180.place_ref
  53.9 1.0 collective-permute-done.10.refs_7_
  54.9 0.2 collective-permute-done.11.refs_8_
  55.2 2.5 %shard_map.116 = (bf16[6,2,128,128]{3,2,1,0:T(8,128)(2,1)}, bf16[10,2,128,128]{3,2,1,0:T(8,128)(2,1)}) custom-call(s32[16]{0:T(128)} %reshape.180.place_ref, bf16[2,2,128,128]{3,2,1,0:T(8,128)(2,1)} %get-tuple-element.11.refs_0_, bf16[2,2,128,128]{3,2,1,0:T(8,128)(2,1)} %copy-done.7, bf16[2,2,128,128]{3,2,1,0:T(8,128)(2,1)} %copy-done.8, ...), custom_call_target="tpu_custom_call" | custom-call | bytes 2097152 | tf_op jit(solution)/shard_map/pallas_call | solution.py:202
  57.6 2.4 %collective-permute-start.12 = (bf16[6,2,128,128]{3,2,1,0:T(8,128)(2,1)}, bf16[6,2,128,128]{3,2,1,0:T(8,128)(2,1)S(1)}, u32[]{:S(2)}, u32[]{:S(2)}) collective-permute-start(bf16[6,2,128,128]{3,2,1,0:T(8,128)(2,1)} %get-tuple-element.12), channel_id=1, source_target_pairs={{0,1},{1,2},{2,3},{3,0},{4,5},{5,6},{6,7},{7,4},{8,9},{9,10},{10,1... | collective-permute-start | bytes 1179656 | tf_op jit(solution)/shard_map/ppermute | solution.py:353
  60.0 1.9 collective-permute-start.13
  61.9 0.7 reduce_max.9
  63.3 0.7 add.187
  64.0 0.1 add.188
  64.2 0.1 add.193
  64.4 0.1 add.181
  64.6 0.1 add.169
  64.8 0.1 add.177
  64.9 2.1 %conditional.1 = (bf16[40,2,128,128]{3,2,1,0:T(8,128)(2,1)}) conditional(s32[]{:T(128)} %convert_element_type.30, () %tuple.14, bf16[10,2,128,128]{3,2,1,0:T(8,128)(2,1)} %get-tuple-element.13), branch_computations={%region_13.14_spmd, %region_14.15_spmd} | conditional | bytes 14418088 | solution.py:449
  64.9 2.1 %broadcast.179 = bf16[40,2,128,128]{3,2,1,0:T(8,128)(2,1)} broadcast(bf16[]{:T(256)} %constant.68.clone), dimensions={} | broadcast | bytes 2621442 | tf_op jit(solution)/shard_map/broadcast.11
  67.0 1.0 constant_dynamic-update-slice_fusion.9
  68.1 2.1 %collective-permute-done.12 = bf16[6,2,128,128]{3,2,1,0:T(8,128)(2,1)S(1)} collective-permute-done((bf16[6,2,128,128]{3,2,1,0:T(8,128)(2,1)}, bf16[6,2,128,128]{3,2,1,0:T(8,128)(2,1)S(1)}, u32[]{:S(2)}, u32[]{:S(2)}) %collective-permute-start.12) | collective-permute-done | bytes 393248 | tf_op jit(solution)/shard_map/ppermute | solution.py:353
  70.2 0.1 collective-permute-start.14
  70.3 2.7 %collective-permute-start.15 = (bf16[3,2,128,128]{3,2,1,0:T(8,128)(2,1)S(1)}, bf16[3,2,128,128]{3,2,1,0:T(8,128)(2,1)S(1)}, u32[]{:S(2)}, u32[]{:S(2)}) collective-permute-start(bf16[3,2,128,128]{3,2,1,0:T(8,128)(2,1)S(1)} %slice.45), channel_id=1, source_target_pairs={{0,3},{1,0},{2,1},{3,2},{4,7},{5,4},{6,5},{7,6},{8,11},{9,8},{10,9... | collective-permute-start | bytes 589832 | tf_op jit(solution)/shard_map/ppermute | solution.py:353
  73.2 8.6 %collective-permute-done.14 = bf16[3,2,128,128]{3,2,1,0:T(8,128)(2,1)S(1)} collective-permute-done((bf16[3,2,128,128]{3,2,1,0:T(8,128)(2,1)S(1)}, bf16[3,2,128,128]{3,2,1,0:T(8,128)(2,1)S(1)}, u32[]{:S(2)}, u32[]{:S(2)}) %collective-permute-start.14) | collective-permute-done | bytes 196640 | tf_op jit(solution)/shard_map/ppermute | solution.py:353
  81.9 1.1 copy-done.1
  83.1 0.1 copy.16
  83.1 0.2 select_reduce_fusion.5
  83.4 0.4 select_reduce_fusion.1
  83.8 0.3 select_reduce_fusion.2
  84.0 0.1 select_reduce_fusion.7
  84.1 0.1 select_reduce_fusion
  84.3 0.1 reshape.179.table_ref
  84.3 0.2 slice_reduce_fusion.length_ref
  84.5 55.7 %all-gather.2.cloned.1.call-done.refs_0_ = bf16[192,2,128,128]{3,2,1,0:T(8,128)(2,1)} async-done(((bf16[6,2,128,128]{3,2,1,0:T(8,128)(2,1)}), bf16[192,2,128,128]{3,2,1,0:T(8,128)(2,1)}) %all-gather.2.cloned.1.call-update) | async-done | bytes 12582928 | tf_op jit(solution)/shard_map/all_gather | solution.py:432
  140.3 1.4 copy-done.2
  141.7 18.4 %shard_map.117 = bf16[8,1024,128]{2,1,0:T(8,128)(2,1)S(1)} custom-call(s32[136]{0:T(256)S(1)} %reshape.179.table_ref, s32[8]{0:T(128)S(1)} %get-tuple-element.14.count_ref, s32[8]{0:T(128)S(1)} %slice_reduce_fusion.length_ref, bf16[8,1296,128]{2,1,0:T(8,128)(2,1)S(1)} %all-to-all-done.in_ref, ...), custom_call_target="tpu_custom_call" | custom-call | flops 4294967296 | bytes 25165824 | tf_op jit(solution)/shard_map/pallas_call | solution.py:321
  160.1 1.3 copy-done
  161.4 5.6 %all-to-all-start.1 = ((bf16[8,1024,128]{2,1,0:T(8,128)(2,1)}), bf16[8,1024,128]{2,1,0:T(8,128)(2,1)}, u32[]{:S(2)}, u32[]{:S(2)}) async-start(bf16[8,1024,128]{2,1,0:T(8,128)(2,1)} %copy-done), calls=%async_computation.1 | async-start | bytes 4194304 | tf_op jit(solution)/shard_map/all_to_all | solution.py:464
  167.0 4.6 %shard_map.113 = bf16[1024,1024]{1,0:T(8,128)(2,1)} custom-call(s32[2]{0:T(128)S(1)} %dynamic_slice.3.blocks_ref, bf16[1024,1024]{1,0:T(8,128)(2,1)S(1)} %copy-done.4, bf16[2,1024,128]{2,1,0:T(8,128)(2,1)S(1)} %copy-done.3), custom_call_target="tpu_custom_call" | custom-call | flops 2147483648 | bytes 5242880 | tf_op jit(solution)/shard_map/pallas_call | solution.py:82
  171.6 21.8 %all-to-all-done.1.in_ref = bf16[8,1024,128]{2,1,0:T(8,128)(2,1)} async-done(((bf16[8,1024,128]{2,1,0:T(8,128)(2,1)}), bf16[8,1024,128]{2,1,0:T(8,128)(2,1)}, u32[]{:S(2)}, u32[]{:S(2)}) %all-to-all-start.1) | async-done | bytes 2097184 | tf_op jit(solution)/shard_map/all_to_all | solution.py:464
  193.4 4.0 %shard_map.118 = bf16[128,8192]{1,0:T(8,128)(2,1)} custom-call(bf16[8,1024,128]{2,1,0:T(8,128)(2,1)} %all-to-all-done.1.in_ref), custom_call_target="tpu_custom_call" | custom-call | bytes 4194304 | tf_op jit(solution)/shard_map/pallas_call | solution.py:140
  (62 shorter events, 1.0 us)
Async XLA Ops:
  7.2 133.1 %all-gather.2.cloned.1.call-start = ((), (), s32[]{:S(2)}) async-start(), calls=%async_computation.2 | async-start | bytes 12976128 | tf_op jit(solution)/shard_map/all_gather | solution.py:432
  9.4 23.2 %collective-permute-start.4 = (bf16[2,2,128,128]{3,2,1,0:T(8,128)(2,1)}, bf16[2,2,128,128]{3,2,1,0:T(8,128)(2,1)S(1)}, u32[]{:S(2)}, u32[]{:S(2)}) collective-permute-start(bf16[2,2,128,128]{3,2,1,0:T(8,128)(2,1)} %get-tuple-element.11.refs_0_), channel_id=1, source_target_pairs={{0,4},{1,5},{2,6},{3,7},{4,8},{5,9},{6,10},{7,11},{8,12},{9,13},{1... | collective-permute-start | bytes 393224 | tf_op jit(solution)/shard_map/ppermute | solution.py:346
  12.1 20.7 %collective-permute-start.5 = (bf16[2,2,128,128]{3,2,1,0:T(8,128)(2,1)}, bf16[2,2,128,128]{3,2,1,0:T(8,128)(2,1)S(1)}, u32[]{:S(2)}, u32[]{:S(2)}) collective-permute-start(bf16[2,2,128,128]{3,2,1,0:T(8,128)(2,1)} %get-tuple-element.11.refs_0_), channel_id=1, source_target_pairs={{0,28},{1,29},{2,30},{3,31},{4,0},{5,1},{6,2},{7,3},{8,4},{9,5},{1... | collective-permute-start | bytes 393224 | tf_op jit(solution)/shard_map/ppermute | solution.py:346
  26.3 5.4 %copy-start.11 = (s32[64]{0:T(128)S(1)}, s32[64]{0:T(128)}, u32[]{:S(2)}) copy-start(s32[64]{0:T(128)} %length_ref.1) | copy-start | bytes 772
  26.3 5.8 %copy-start.14 = (s32[8]{0:T(128)S(1)}, s32[8]{0:T(128)}, u32[]{:S(2)}) copy-start(s32[8]{0:T(128)} %constant.96) | copy-start | bytes 100
  26.3 9.2 %copy-start.13 = (s32[4]{0:T(128)S(1)}, s32[4]{0:T(128)}, u32[]{:S(2)}) copy-start(s32[4]{0:T(128)} %constant.86.clone) | copy-start | bytes 52
  26.3 56.8 %all-to-all-start = ((bf16[8,1296,128]{2,1,0:T(8,128)(2,1)}), bf16[8,1296,128]{2,1,0:T(8,128)(2,1)S(1)}, u32[]{:S(2)}, u32[]{:S(2)}) async-start(bf16[8,1296,128]{2,1,0:T(8,128)(2,1)} %shard_map.114), calls=%async_computation | async-start | bytes 5308416 | tf_op jit(solution)/shard_map/all_to_all | solution.py:438
  32.6 22.5 %copy-start.7 = (bf16[2,2,128,128]{3,2,1,0:T(8,128)(2,1)}, bf16[2,2,128,128]{3,2,1,0:T(8,128)(2,1)S(1)}, u32[]{:S(2)}) copy-start(bf16[2,2,128,128]{3,2,1,0:T(8,128)(2,1)S(1)} %collective-permute-done.4.refs_1_) | copy-start | bytes 393220
  32.6 8.5 %collective-permute-start.6 = (bf16[2,2,128,128]{3,2,1,0:T(8,128)(2,1)S(1)}, bf16[2,2,128,128]{3,2,1,0:T(8,128)(2,1)S(1)}, u32[]{:S(2)}, u32[]{:S(2)}) collective-permute-start(bf16[2,2,128,128]{3,2,1,0:T(8,128)(2,1)S(1)} %collective-permute-done.4.refs_1_), channel_id=1, source_target_pairs={{0,4},{1,5},{2,6},{3,7},{4,8},{5,9},{6,10},{7,11},{8,12},{9,13},{1... | collective-permute-start | bytes 393224 | tf_op jit(solution)/shard_map/ppermute | solution.py:346
  32.7 22.4 %copy-start.8 = (bf16[2,2,128,128]{3,2,1,0:T(8,128)(2,1)}, bf16[2,2,128,128]{3,2,1,0:T(8,128)(2,1)S(1)}, u32[]{:S(2)}) copy-start(bf16[2,2,128,128]{3,2,1,0:T(8,128)(2,1)S(1)} %collective-permute-done.5.refs_2_) | copy-start | bytes 393220
  32.7 8.4 %collective-permute-start.7 = (bf16[2,2,128,128]{3,2,1,0:T(8,128)(2,1)S(1)}, bf16[2,2,128,128]{3,2,1,0:T(8,128)(2,1)S(1)}, u32[]{:S(2)}, u32[]{:S(2)}) collective-permute-start(bf16[2,2,128,128]{3,2,1,0:T(8,128)(2,1)S(1)} %collective-permute-done.5.refs_2_), channel_id=1, source_target_pairs={{0,28},{1,29},{2,30},{3,31},{4,0},{5,1},{6,2},{7,3},{8,4},{9,5},{1... | collective-permute-start | bytes 393224 | tf_op jit(solution)/shard_map/ppermute | solution.py:346
  41.1 14.0 %copy-start.9 = (bf16[2,2,128,128]{3,2,1,0:T(8,128)(2,1)}, bf16[2,2,128,128]{3,2,1,0:T(8,128)(2,1)S(1)}, u32[]{:S(2)}) copy-start(bf16[2,2,128,128]{3,2,1,0:T(8,128)(2,1)S(1)} %collective-permute-done.6.refs_3_) | copy-start | bytes 393220
  41.1 8.4 %collective-permute-start.8 = (bf16[2,2,128,128]{3,2,1,0:T(8,128)(2,1)S(1)}, bf16[2,2,128,128]{3,2,1,0:T(8,128)(2,1)S(1)}, u32[]{:S(2)}, u32[]{:S(2)}) collective-permute-start(bf16[2,2,128,128]{3,2,1,0:T(8,128)(2,1)S(1)} %collective-permute-done.6.refs_3_), channel_id=1, source_target_pairs={{0,4},{1,5},{2,6},{3,7},{4,8},{5,9},{6,10},{7,11},{8,12},{9,13},{1... | collective-permute-start | bytes 393224 | tf_op jit(solution)/shard_map/ppermute | solution.py:346
  41.1 14.0 %copy-start.10 = (bf16[2,2,128,128]{3,2,1,0:T(8,128)(2,1)}, bf16[2,2,128,128]{3,2,1,0:T(8,128)(2,1)S(1)}, u32[]{:S(2)}) copy-start(bf16[2,2,128,128]{3,2,1,0:T(8,128)(2,1)S(1)} %collective-permute-done.7.refs_4_) | copy-start | bytes 393220
  41.1 8.5 %collective-permute-start.9 = (bf16[2,2,128,128]{3,2,1,0:T(8,128)(2,1)S(1)}, bf16[2,2,128,128]{3,2,1,0:T(8,128)(2,1)S(1)}, u32[]{:S(2)}, u32[]{:S(2)}) collective-permute-start(bf16[2,2,128,128]{3,2,1,0:T(8,128)(2,1)S(1)} %collective-permute-done.7.refs_4_), channel_id=1, source_target_pairs={{0,28},{1,29},{2,30},{3,31},{4,0},{5,1},{6,2},{7,3},{8,4},{9,5},{1... | collective-permute-start | bytes 393224 | tf_op jit(solution)/shard_map/ppermute | solution.py:346
  49.6 5.6 %copy-start.5 = (bf16[2,2,128,128]{3,2,1,0:T(8,128)(2,1)}, bf16[2,2,128,128]{3,2,1,0:T(8,128)(2,1)S(1)}, u32[]{:S(2)}) copy-start(bf16[2,2,128,128]{3,2,1,0:T(8,128)(2,1)S(1)} %collective-permute-done.8.refs_5_) | copy-start | bytes 393220
  49.6 5.3 %collective-permute-start.10 = (bf16[1,2,128,128]{3,2,1,0:T(8,128)(2,1)S(1)}, bf16[1,2,128,128]{3,2,1,0:T(8,128)(2,1)}, u32[]{:S(2)}, u32[]{:S(2)}) collective-permute-start(bf16[1,2,128,128]{3,2,1,0:T(8,128)(2,1)S(1)} %slice.42), channel_id=1, source_target_pairs={{0,4},{1,5},{2,6},{3,7},{4,8},{5,9},{6,10},{7,11},{8,12},{9,13},{1... | collective-permute-start | bytes 196616 | tf_op jit(solution)/shard_map/ppermute | solution.py:346
  49.7 5.5 %copy-start.6 = (bf16[2,2,128,128]{3,2,1,0:T(8,128)(2,1)}, bf16[2,2,128,128]{3,2,1,0:T(8,128)(2,1)S(1)}, u32[]{:S(2)}) copy-start(bf16[2,2,128,128]{3,2,1,0:T(8,128)(2,1)S(1)} %collective-permute-done.9.refs_6_) | copy-start | bytes 393220
  50.3 4.8 %collective-permute-start.11 = (bf16[1,2,128,128]{3,2,1,0:T(8,128)(2,1)}, bf16[1,2,128,128]{3,2,1,0:T(8,128)(2,1)}, u32[]{:S(2)}, u32[]{:S(2)}) collective-permute-start(bf16[1,2,128,128]{3,2,1,0:T(8,128)(2,1)} %slice.43), channel_id=1, source_target_pairs={{0,28},{1,29},{2,30},{3,31},{4,0},{5,1},{6,2},{7,3},{8,4},{9,5},{1... | collective-permute-start | bytes 196616 | tf_op jit(solution)/shard_map/ppermute | solution.py:346
  57.6 12.6 %collective-permute-start.12 = (bf16[6,2,128,128]{3,2,1,0:T(8,128)(2,1)}, bf16[6,2,128,128]{3,2,1,0:T(8,128)(2,1)S(1)}, u32[]{:S(2)}, u32[]{:S(2)}) collective-permute-start(bf16[6,2,128,128]{3,2,1,0:T(8,128)(2,1)} %get-tuple-element.12), channel_id=1, source_target_pairs={{0,1},{1,2},{2,3},{3,0},{4,5},{5,6},{6,7},{7,4},{8,9},{9,10},{10,1... | collective-permute-start | bytes 1179656 | tf_op jit(solution)/shard_map/ppermute | solution.py:353
  60.0 10.3 %collective-permute-start.13 = (bf16[6,2,128,128]{3,2,1,0:T(8,128)(2,1)}, bf16[6,2,128,128]{3,2,1,0:T(8,128)(2,1)S(1)}, u32[]{:S(2)}, u32[]{:S(2)}) collective-permute-start(bf16[6,2,128,128]{3,2,1,0:T(8,128)(2,1)} %get-tuple-element.12), channel_id=1, source_target_pairs={{0,3},{1,0},{2,1},{3,2},{4,7},{5,4},{6,5},{7,6},{8,11},{9,8},{10,9... | collective-permute-start | bytes 1179656 | tf_op jit(solution)/shard_map/ppermute | solution.py:353
  67.0 16.1 %copy-start.12 = (s32[64]{0:T(128)S(1)}, s32[64]{0:T(128)}, u32[]{:S(2)}) copy-start(s32[64]{0:T(128)} %param.15) | copy-start | bytes 772
  70.2 11.6 %collective-permute-start.14 = (bf16[3,2,128,128]{3,2,1,0:T(8,128)(2,1)S(1)}, bf16[3,2,128,128]{3,2,1,0:T(8,128)(2,1)S(1)}, u32[]{:S(2)}, u32[]{:S(2)}) collective-permute-start(bf16[3,2,128,128]{3,2,1,0:T(8,128)(2,1)S(1)} %slice.44), channel_id=1, source_target_pairs={{0,1},{1,2},{2,3},{3,0},{4,5},{5,6},{6,7},{7,4},{8,9},{9,10},{10,1... | collective-permute-start | bytes 589832 | tf_op jit(solution)/shard_map/ppermute | solution.py:353
  70.3 11.5 %collective-permute-start.15 = (bf16[3,2,128,128]{3,2,1,0:T(8,128)(2,1)S(1)}, bf16[3,2,128,128]{3,2,1,0:T(8,128)(2,1)S(1)}, u32[]{:S(2)}, u32[]{:S(2)}) collective-permute-start(bf16[3,2,128,128]{3,2,1,0:T(8,128)(2,1)S(1)} %slice.45), channel_id=1, source_target_pairs={{0,3},{1,0},{2,1},{3,2},{4,7},{5,4},{6,5},{7,6},{8,11},{9,8},{10,9... | collective-permute-start | bytes 589832 | tf_op jit(solution)/shard_map/ppermute | solution.py:353
  81.9 1.1 copy-start.1
  140.3 1.4 copy-start.2
  160.1 1.3 copy-start
  161.4 5.6 %copy-start.3 = (bf16[2,1024,128]{2,1,0:T(8,128)(2,1)S(1)}, bf16[2,1024,128]{2,1,0:T(8,128)(2,1)}, u32[]{:S(2)}) copy-start(bf16[2,1024,128]{2,1,0:T(8,128)(2,1)} %kv_ref.3) | copy-start | bytes 1572868
  161.4 5.6 %copy-start.4 = (bf16[1024,1024]{1,0:T(8,128)(2,1)S(1)}, bf16[1024,1024]{1,0:T(8,128)(2,1)}, u32[]{:S(2)}) copy-start(bf16[1024,1024]{1,0:T(8,128)(2,1)} %q_ref.2) | copy-start | bytes 6291460
  161.4 32.0 %all-to-all-start.1 = ((bf16[8,1024,128]{2,1,0:T(8,128)(2,1)}), bf16[8,1024,128]{2,1,0:T(8,128)(2,1)}, u32[]{:S(2)}, u32[]{:S(2)}) async-start(bf16[8,1024,128]{2,1,0:T(8,128)(2,1)} %copy-done), calls=%async_computation.1 | async-start | bytes 4194304 | tf_op jit(solution)/shard_map/all_to_all | solution.py:464
Sparse Core Ops, SparseCore 0:
  11.1 129.0 all-gather.1

commit v3 on v2

--- a/solution.py
+++ b/solution.py
@@ -135,7 +135,7 @@
 
 
 def spread(answer):
-    groups = 2
+    groups = 4
     width = groups * GROUP * HEAD_SIZE
     return pl.pallas_call(
         spread_kernel,
@@ -320,12 +320,12 @@
     requests = payload.shape[0]
     return pl.pallas_call(
         question_kernel,
-        out_shape=jax.ShapeDtypeStruct((requests, OWN_ROW, HEAD_SIZE), jnp.bfloat16),
+        out_shape=pltpu.HBM((requests, OWN_ROW, HEAD_SIZE), jnp.bfloat16),
         grid_spec=pltpu.PrefetchScalarGridSpec(
             num_scalar_prefetch=3,
             grid=(requests,),
             in_specs=[pl.BlockSpec((1, PAYLOAD, HEAD_SIZE), lambda r, *_: (r, 0, 0))]
-            + [pl.BlockSpec(memory_space=pl.ANY)] * len(pieces),
+            + [pl.BlockSpec(memory_space=pltpu.HBM)] * len(pieces),
             out_specs=pl.BlockSpec((1, OWN_ROW, HEAD_SIZE), lambda r, *_: (r, 0, 0)),
             scratch_shapes=[
                 pltpu.VMEM((requests, MOST + 1, *pieces[0].shape[1:]), jnp.bfloat16),

time: 207 us -> 204 us (0.986)
  Pallas kernels: 37.7 us -> 35.5 us
    unnamed x35 -> x33, local copies, waits for them, and re-layouts: 7.03 us -> 5.72 us
  transfers between devices with their start and end apart: 15 -> 15, of which waited for: 8 -> 8; matrix products, arithmetic and copies ran while one was open for 7% -> 7% of each run, Pallas kernels for 6% -> 7%
where the time goes in v3:
time: 204 us; the launch traced here: 201 us
  waiting for transfers between devices  100 us (49%)
  Pallas kernels  35.5 us (17%)
  starting transfers between devices  33.2 us (16%)
  between operations  15.7 us (8%)
  local copies, waits for them, and re-layouts  11.6 us (6%)
  other arithmetic  4.58 us (2%)
    all_gather x1, waiting for transfers between devices, body(): pieces = [lax.all_gather(kept, 'work', axis=0, tiled=True)]  56.8 us
    all_to_all x1, waiting for transfers between devices, body(): answer = lax.all_to_all(answer, 'req', 0, 0, tiled=True)  21.8 us
    pallas_call x1, Pallas kernels, question_attention(): pl.pallas_call(question_kernel, out_shape=pltpu.HBM((requests, OWN_ROW, H...  17.4 us
    ppermute x8, starting transfers between devices, step_z(): return lax.ppermute(array, 'work', steps)  15 us
    ppermute x8, waiting for transfers between devices, step_z(): return lax.ppermute(array, 'work', steps)  11.4 us
    ppermute x4, waiting for transfers between devices, step_y(): return lax.ppermute(array, 'work', steps)  9.98 us
    ppermute x4, starting transfers between devices, step_y(): return lax.ppermute(array, 'work', steps)  7.28 us
    pallas_call x1, Pallas kernels, bundle(): pl.pallas_call(bundle_kernel, out_shape=jax.ShapeDtypeStruct((KEY_VALUE_H...  6.1 us
  transfers between devices with their start and end apart: 15, of which 8 were waited for; matrix products, arithmetic and copies ran while one was open for 7% of the time, Pallas kernels for 7%

profile of v3, /device:TPU:1, one launch (start us, length us, event | category | flops | bytes accessed | tf_op | source)
XLA Modules:
  0.0 200.6 jit_solution(2516464391771454531)
XLA Ops:
  7.2 2.2 %shard_map.115 = (bf16[6,2,128,128]{3,2,1,0:T(8,128)(2,1)}, bf16[2,2,128,128]{3,2,1,0:T(8,128)(2,1)}) custom-call(s32[64]{0:T(128)} %length_ref.1, bf16[2,1024,128]{2,1,0:T(8,128)(2,1)} %kv_ref.3), custom_call_target="tpu_custom_call" | custom-call | bytes 1048576 | tf_op jit(solution)/shard_map/pallas_call | solution.py:177
  9.4 2.6 %collective-permute-start.4 = (bf16[2,2,128,128]{3,2,1,0:T(8,128)(2,1)}, bf16[2,2,128,128]{3,2,1,0:T(8,128)(2,1)S(1)}, u32[]{:S(2)}, u32[]{:S(2)}) collective-permute-start(bf16[2,2,128,128]{3,2,1,0:T(8,128)(2,1)} %get-tuple-element.11.refs_0_), channel_id=1, source_target_pairs={{0,4},{1,5},{2,6},{3,7},{4,8},{5,9},{6,10},{7,11},{8,12},{9,13},{1... | collective-permute-start | bytes 393224 | tf_op jit(solution)/shard_map/ppermute | solution.py:346
  12.0 4.1 %collective-permute-start.5 = (bf16[2,2,128,128]{3,2,1,0:T(8,128)(2,1)}, bf16[2,2,128,128]{3,2,1,0:T(8,128)(2,1)S(1)}, u32[]{:S(2)}, u32[]{:S(2)}) collective-permute-start(bf16[2,2,128,128]{3,2,1,0:T(8,128)(2,1)} %get-tuple-element.11.refs_0_), channel_id=1, source_target_pairs={{0,28},{1,29},{2,30},{3,31},{4,0},{5,1},{6,2},{7,3},{8,4},{9,5},{1... | collective-permute-start | bytes 393224 | tf_op jit(solution)/shard_map/ppermute | solution.py:346
  16.1 2.0 copy.21
  18.7 0.7 convert.8
  19.4 0.7 fusion.5.facts_ref
  20.0 6.1 %shard_map.114 = bf16[8,1296,128]{2,1,0:T(8,128)(2,1)} custom-call(bf16[128,8192]{1,0:T(8,128)(2,1)} %q_ref.3, bf16[128,2048]{1,0:T(8,128)(2,1)} %bitcast.6, bf16[128,2048]{1,0:T(8,128)(2,1)} %bitcast.7, bf16[16,128]{1,0:T(8,128)(2,1)} %fusion.5.facts_ref), custom_call_target="tpu_custom_call" | custom-call | bytes 5242880 | tf_op jit(solution)/shard_map/pallas_call | solution.py:113
  26.1 5.4 %all-to-all-start = ((bf16[8,1296,128]{2,1,0:T(8,128)(2,1)}), bf16[8,1296,128]{2,1,0:T(8,128)(2,1)S(1)}, u32[]{:S(2)}, u32[]{:S(2)}) async-start(bf16[8,1296,128]{2,1,0:T(8,128)(2,1)} %shard_map.114), calls=%async_computation | async-start | bytes 5308416 | tf_op jit(solution)/shard_map/all_to_all | solution.py:438
  31.5 0.1 reshape.178
  31.6 0.2 reduce_sum.111
  32.0 0.1 copy.17
  32.0 0.1 multiply_reduce_fusion
  32.3 0.1 copy.18
  32.4 0.1 select_reduce_fusion.4
  32.5 0.1 collective-permute-start.6
  32.6 2.6 %collective-permute-start.7 = (bf16[2,2,128,128]{3,2,1,0:T(8,128)(2,1)S(1)}, bf16[2,2,128,128]{3,2,1,0:T(8,128)(2,1)S(1)}, u32[]{:S(2)}, u32[]{:S(2)}) collective-permute-start(bf16[2,2,128,128]{3,2,1,0:T(8,128)(2,1)S(1)} %collective-permute-done.5.refs_2_), channel_id=1, source_target_pairs={{0,28},{1,29},{2,30},{3,31},{4,0},{5,1},{6,2},{7,3},{8,4},{9,5},{1... | collective-permute-start | bytes 393224 | tf_op jit(solution)/shard_map/ppermute | solution.py:346
  35.3 0.1 copy.19
  35.3 0.2 select_reduce_fusion.8
  35.5 5.7 %collective-permute-done.6.refs_3_ = bf16[2,2,128,128]{3,2,1,0:T(8,128)(2,1)S(1)} collective-permute-done((bf16[2,2,128,128]{3,2,1,0:T(8,128)(2,1)S(1)}, bf16[2,2,128,128]{3,2,1,0:T(8,128)(2,1)S(1)}, u32[]{:S(2)}, u32[]{:S(2)}) %collective-permute-start.6) | collective-permute-done | bytes 131104 | tf_op jit(solution)/shard_map/ppermute | solution.py:346
  41.2 2.7 %collective-permute-start.9 = (bf16[2,2,128,128]{3,2,1,0:T(8,128)(2,1)S(1)}, bf16[2,2,128,128]{3,2,1,0:T(8,128)(2,1)S(1)}, u32[]{:S(2)}, u32[]{:S(2)}) collective-permute-start(bf16[2,2,128,128]{3,2,1,0:T(8,128)(2,1)S(1)} %collective-permute-done.7.refs_4_), channel_id=1, source_target_pairs={{0,28},{1,29},{2,30},{3,31},{4,0},{5,1},{6,2},{7,3},{8,4},{9,5},{1... | collective-permute-start | bytes 393224 | tf_op jit(solution)/shard_map/ppermute | solution.py:346
  43.9 0.5 multiply_add_fusion.1
  44.4 4.5 %collective-permute-done.8.refs_5_ = bf16[2,2,128,128]{3,2,1,0:T(8,128)(2,1)S(1)} collective-permute-done((bf16[2,2,128,128]{3,2,1,0:T(8,128)(2,1)S(1)}, bf16[2,2,128,128]{3,2,1,0:T(8,128)(2,1)S(1)}, u32[]{:S(2)}, u32[]{:S(2)}) %collective-permute-start.8) | collective-permute-done | bytes 131104 | tf_op jit(solution)/shard_map/ppermute | solution.py:346
  48.9 0.1 collective-permute-start.10
  49.0 0.7 slice.43
  49.7 2.9 %collective-permute-start.11 = (bf16[1,2,128,128]{3,2,1,0:T(8,128)(2,1)}, bf16[1,2,128,128]{3,2,1,0:T(8,128)(2,1)}, u32[]{:S(2)}, u32[]{:S(2)}) collective-permute-start(bf16[1,2,128,128]{3,2,1,0:T(8,128)(2,1)} %slice.43), channel_id=1, source_target_pairs={{0,28},{1,29},{2,30},{3,31},{4,0},{5,1},{6,2},{7,3},{8,4},{9,5},{1... | collective-permute-start | bytes 196616 | tf_op jit(solution)/shard_map/ppermute | solution.py:346
  52.6 0.1 select_reduce_fusion.6
  52.7 0.1 copy.20
  52.8 0.7 reshape.180.place_ref
  53.5 0.4 collective-permute-done.10.refs_7_
  53.9 0.8 collective-permute-done.11.refs_8_
  54.7 2.5 %shard_map.116 = (bf16[6,2,128,128]{3,2,1,0:T(8,128)(2,1)}, bf16[10,2,128,128]{3,2,1,0:T(8,128)(2,1)}) custom-call(s32[16]{0:T(128)} %reshape.180.place_ref, bf16[2,2,128,128]{3,2,1,0:T(8,128)(2,1)} %get-tuple-element.11.refs_0_, bf16[2,2,128,128]{3,2,1,0:T(8,128)(2,1)} %copy-done.6, bf16[2,2,128,128]{3,2,1,0:T(8,128)(2,1)} %copy-done.7, ...), custom_call_target="tpu_custom_call" | custom-call | bytes 2097152 | tf_op jit(solution)/shard_map/pallas_call | solution.py:202
  57.1 1.9 collective-permute-start.12
  59.0 2.6 %collective-permute-start.13 = (bf16[6,2,128,128]{3,2,1,0:T(8,128)(2,1)}, bf16[6,2,128,128]{3,2,1,0:T(8,128)(2,1)S(1)}, u32[]{:S(2)}, u32[]{:S(2)}) collective-permute-start(bf16[6,2,128,128]{3,2,1,0:T(8,128)(2,1)} %get-tuple-element.12), channel_id=1, source_target_pairs={{0,3},{1,0},{2,1},{3,2},{4,7},{5,4},{6,5},{7,6},{8,11},{9,8},{10,9... | collective-permute-start | bytes 1179656 | tf_op jit(solution)/shard_map/ppermute | solution.py:353
  61.6 0.7 reduce_max.9
  62.9 0.7 add.187
  63.6 0.1 add.188
  63.8 0.1 add.193
  64.0 0.1 add.181
  64.1 0.1 concatenate.25
  64.2 0.1 add.169
  64.4 0.1 add.177
  64.5 2.1 %conditional.1 = (bf16[40,2,128,128]{3,2,1,0:T(8,128)(2,1)}) conditional(s32[]{:T(128)} %convert_element_type.30, () %tuple.14, bf16[10,2,128,128]{3,2,1,0:T(8,128)(2,1)} %get-tuple-element.13), branch_computations={%region_13.14_spmd, %region_14.15_spmd} | conditional | bytes 14418088 | solution.py:449
  64.5 2.1 %broadcast.179 = bf16[40,2,128,128]{3,2,1,0:T(8,128)(2,1)} broadcast(bf16[]{:T(256)} %constant.68.clone), dimensions={} | broadcast | bytes 2621442 | tf_op jit(solution)/shard_map/broadcast.11
  66.6 1.0 constant_dynamic-update-slice_fusion.9
  67.7 1.8 collective-permute-done.12
  69.5 0.1 collective-permute-start.14
  69.6 2.7 %collective-permute-start.15 = (bf16[3,2,128,128]{3,2,1,0:T(8,128)(2,1)S(1)}, bf16[3,2,128,128]{3,2,1,0:T(8,128)(2,1)S(1)}, u32[]{:S(2)}, u32[]{:S(2)}) collective-permute-start(bf16[3,2,128,128]{3,2,1,0:T(8,128)(2,1)S(1)} %slice.45), channel_id=1, source_target_pairs={{0,3},{1,0},{2,1},{3,2},{4,7},{5,4},{6,5},{7,6},{8,11},{9,8},{10,9... | collective-permute-start | bytes 589832 | tf_op jit(solution)/shard_map/ppermute | solution.py:353
  72.4 8.2 %collective-permute-done.14 = bf16[3,2,128,128]{3,2,1,0:T(8,128)(2,1)S(1)} collective-permute-done((bf16[3,2,128,128]{3,2,1,0:T(8,128)(2,1)S(1)}, bf16[3,2,128,128]{3,2,1,0:T(8,128)(2,1)S(1)}, u32[]{:S(2)}, u32[]{:S(2)}) %collective-permute-start.14) | collective-permute-done | bytes 196640 | tf_op jit(solution)/shard_map/ppermute | solution.py:353
  80.7 1.1 copy-done
  81.9 0.1 copy.16
  82.0 0.2 select_reduce_fusion.5
  82.2 0.4 select_reduce_fusion.1
  82.6 0.3 select_reduce_fusion.2
  82.9 0.1 select_reduce_fusion.7
  83.0 0.1 select_reduce_fusion
  83.1 0.1 reshape.179.table_ref
  83.2 0.2 slice_reduce_fusion.length_ref
  83.3 56.8 %all-gather.2.cloned.1.call-done.refs_0_ = bf16[192,2,128,128]{3,2,1,0:T(8,128)(2,1)} async-done(((bf16[6,2,128,128]{3,2,1,0:T(8,128)(2,1)}), bf16[192,2,128,128]{3,2,1,0:T(8,128)(2,1)}) %all-gather.2.cloned.1.call-update) | async-done | bytes 12582928 | tf_op jit(solution)/shard_map/all_gather | solution.py:432
  140.2 1.4 copy-done.1
  141.6 17.4 %shard_map.117 = bf16[8,1024,128]{2,1,0:T(8,128)(2,1)} custom-call(s32[136]{0:T(256)S(1)} %reshape.179.table_ref, s32[8]{0:T(128)S(1)} %get-tuple-element.14.count_ref, s32[8]{0:T(128)S(1)} %slice_reduce_fusion.length_ref, bf16[8,1296,128]{2,1,0:T(8,128)(2,1)S(1)} %all-to-all-done.in_ref, bf16[192,2,128,128]{3,2,1,0:T(8,128)(2,1)} %all-gather.2.cloned.1.call-done.refs_0_, ...), custom_call_target="tpu_custom_call" | custom-call | flops 4294967296 | bytes 25165824 | tf_op jit(solution)/shard_map/pallas_call | solution.py:321
  159.0 5.5 %all-to-all-start.1 = ((bf16[8,1024,128]{2,1,0:T(8,128)(2,1)}), bf16[8,1024,128]{2,1,0:T(8,128)(2,1)}, u32[]{:S(2)}, u32[]{:S(2)}) async-start(bf16[8,1024,128]{2,1,0:T(8,128)(2,1)} %shard_map.117), calls=%async_computation.1 | async-start | bytes 4194304 | tf_op jit(solution)/shard_map/all_to_all | solution.py:464
  164.5 4.6 %shard_map.113 = bf16[1024,1024]{1,0:T(8,128)(2,1)} custom-call(s32[2]{0:T(128)S(1)} %dynamic_slice.3.blocks_ref, bf16[1024,1024]{1,0:T(8,128)(2,1)S(1)} %copy-done.3, bf16[2,1024,128]{2,1,0:T(8,128)(2,1)S(1)} %copy-done.2), custom_call_target="tpu_custom_call" | custom-call | flops 2147483648 | bytes 5242880 | tf_op jit(solution)/shard_map/pallas_call | solution.py:82
  169.1 21.8 %all-to-all-done.1.in_ref = bf16[8,1024,128]{2,1,0:T(8,128)(2,1)} async-done(((bf16[8,1024,128]{2,1,0:T(8,128)(2,1)}), bf16[8,1024,128]{2,1,0:T(8,128)(2,1)}, u32[]{:S(2)}, u32[]{:S(2)}) %all-to-all-start.1) | async-done | bytes 2097184 | tf_op jit(solution)/shard_map/all_to_all | solution.py:464
  190.9 2.8 %shard_map.118 = bf16[128,8192]{1,0:T(8,128)(2,1)} custom-call(bf16[8,1024,128]{2,1,0:T(8,128)(2,1)} %all-to-all-done.1.in_ref), custom_call_target="tpu_custom_call" | custom-call | bytes 4194304 | tf_op jit(solution)/shard_map/pallas_call | solution.py:140
  (60 shorter events, 0.9 us)
Async XLA Ops:
  7.2 133.0 %all-gather.2.cloned.1.call-start = ((), (), s32[]{:S(2)}) async-start(), calls=%async_computation.2 | async-start | bytes 12976128 | tf_op jit(solution)/shard_map/all_gather | solution.py:432
  9.4 23.1 %collective-permute-start.4 = (bf16[2,2,128,128]{3,2,1,0:T(8,128)(2,1)}, bf16[2,2,128,128]{3,2,1,0:T(8,128)(2,1)S(1)}, u32[]{:S(2)}, u32[]{:S(2)}) collective-permute-start(bf16[2,2,128,128]{3,2,1,0:T(8,128)(2,1)} %get-tuple-element.11.refs_0_), channel_id=1, source_target_pairs={{0,4},{1,5},{2,6},{3,7},{4,8},{5,9},{6,10},{7,11},{8,12},{9,13},{1... | collective-permute-start | bytes 393224 | tf_op jit(solution)/shard_map/ppermute | solution.py:346
  12.0 20.6 %collective-permute-start.5 = (bf16[2,2,128,128]{3,2,1,0:T(8,128)(2,1)}, bf16[2,2,128,128]{3,2,1,0:T(8,128)(2,1)S(1)}, u32[]{:S(2)}, u32[]{:S(2)}) collective-permute-start(bf16[2,2,128,128]{3,2,1,0:T(8,128)(2,1)} %get-tuple-element.11.refs_0_), channel_id=1, source_target_pairs={{0,28},{1,29},{2,30},{3,31},{4,0},{5,1},{6,2},{7,3},{8,4},{9,5},{1... | collective-permute-start | bytes 393224 | tf_op jit(solution)/shard_map/ppermute | solution.py:346
  26.1 5.4 %copy-start.10 = (s32[64]{0:T(128)S(1)}, s32[64]{0:T(128)}, u32[]{:S(2)}) copy-start(s32[64]{0:T(128)} %length_ref.1) | copy-start | bytes 772
  26.1 5.8 %copy-start.13 = (s32[8]{0:T(128)S(1)}, s32[8]{0:T(128)}, u32[]{:S(2)}) copy-start(s32[8]{0:T(128)} %constant.96) | copy-start | bytes 100
  26.1 9.2 %copy-start.12 = (s32[4]{0:T(128)S(1)}, s32[4]{0:T(128)}, u32[]{:S(2)}) copy-start(s32[4]{0:T(128)} %constant.86.clone) | copy-start | bytes 52
  26.1 55.7 %all-to-all-start = ((bf16[8,1296,128]{2,1,0:T(8,128)(2,1)}), bf16[8,1296,128]{2,1,0:T(8,128)(2,1)S(1)}, u32[]{:S(2)}, u32[]{:S(2)}) async-start(bf16[8,1296,128]{2,1,0:T(8,128)(2,1)} %shard_map.114), calls=%async_computation | async-start | bytes 5308416 | tf_op jit(solution)/shard_map/all_to_all | solution.py:438
  32.5 22.2 %copy-start.6 = (bf16[2,2,128,128]{3,2,1,0:T(8,128)(2,1)}, bf16[2,2,128,128]{3,2,1,0:T(8,128)(2,1)S(1)}, u32[]{:S(2)}) copy-start(bf16[2,2,128,128]{3,2,1,0:T(8,128)(2,1)S(1)} %collective-permute-done.4.refs_1_) | copy-start | bytes 393220
  32.5 8.7 %collective-permute-start.6 = (bf16[2,2,128,128]{3,2,1,0:T(8,128)(2,1)S(1)}, bf16[2,2,128,128]{3,2,1,0:T(8,128)(2,1)S(1)}, u32[]{:S(2)}, u32[]{:S(2)}) collective-permute-start(bf16[2,2,128,128]{3,2,1,0:T(8,128)(2,1)S(1)} %collective-permute-done.4.refs_1_), channel_id=1, source_target_pairs={{0,4},{1,5},{2,6},{3,7},{4,8},{5,9},{6,10},{7,11},{8,12},{9,13},{1... | collective-permute-start | bytes 393224 | tf_op jit(solution)/shard_map/ppermute | solution.py:346
  32.6 22.1 %copy-start.7 = (bf16[2,2,128,128]{3,2,1,0:T(8,128)(2,1)}, bf16[2,2,128,128]{3,2,1,0:T(8,128)(2,1)S(1)}, u32[]{:S(2)}) copy-start(bf16[2,2,128,128]{3,2,1,0:T(8,128)(2,1)S(1)} %collective-permute-done.5.refs_2_) | copy-start | bytes 393220
  32.6 8.6 %collective-permute-start.7 = (bf16[2,2,128,128]{3,2,1,0:T(8,128)(2,1)S(1)}, bf16[2,2,128,128]{3,2,1,0:T(8,128)(2,1)S(1)}, u32[]{:S(2)}, u32[]{:S(2)}) collective-permute-start(bf16[2,2,128,128]{3,2,1,0:T(8,128)(2,1)S(1)} %collective-permute-done.5.refs_2_), channel_id=1, source_target_pairs={{0,28},{1,29},{2,30},{3,31},{4,0},{5,1},{6,2},{7,3},{8,4},{9,5},{1... | collective-permute-start | bytes 393224 | tf_op jit(solution)/shard_map/ppermute | solution.py:346
  41.2 13.4 %copy-start.8 = (bf16[2,2,128,128]{3,2,1,0:T(8,128)(2,1)}, bf16[2,2,128,128]{3,2,1,0:T(8,128)(2,1)S(1)}, u32[]{:S(2)}) copy-start(bf16[2,2,128,128]{3,2,1,0:T(8,128)(2,1)S(1)} %collective-permute-done.6.refs_3_) | copy-start | bytes 393220
  41.2 7.7 %collective-permute-start.8 = (bf16[2,2,128,128]{3,2,1,0:T(8,128)(2,1)S(1)}, bf16[2,2,128,128]{3,2,1,0:T(8,128)(2,1)S(1)}, u32[]{:S(2)}, u32[]{:S(2)}) collective-permute-start(bf16[2,2,128,128]{3,2,1,0:T(8,128)(2,1)S(1)} %collective-permute-done.6.refs_3_), channel_id=1, source_target_pairs={{0,4},{1,5},{2,6},{3,7},{4,8},{5,9},{6,10},{7,11},{8,12},{9,13},{1... | collective-permute-start | bytes 393224 | tf_op jit(solution)/shard_map/ppermute | solution.py:346
  41.2 13.4 %copy-start.9 = (bf16[2,2,128,128]{3,2,1,0:T(8,128)(2,1)}, bf16[2,2,128,128]{3,2,1,0:T(8,128)(2,1)S(1)}, u32[]{:S(2)}) copy-start(bf16[2,2,128,128]{3,2,1,0:T(8,128)(2,1)S(1)} %collective-permute-done.7.refs_4_) | copy-start | bytes 393220
  41.2 7.8 %collective-permute-start.9 = (bf16[2,2,128,128]{3,2,1,0:T(8,128)(2,1)S(1)}, bf16[2,2,128,128]{3,2,1,0:T(8,128)(2,1)S(1)}, u32[]{:S(2)}, u32[]{:S(2)}) collective-permute-start(bf16[2,2,128,128]{3,2,1,0:T(8,128)(2,1)S(1)} %collective-permute-done.7.refs_4_), channel_id=1, source_target_pairs={{0,28},{1,29},{2,30},{3,31},{4,0},{5,1},{6,2},{7,3},{8,4},{9,5},{1... | collective-permute-start | bytes 393224 | tf_op jit(solution)/shard_map/ppermute | solution.py:346
  48.9 5.7 %copy-start.4 = (bf16[2,2,128,128]{3,2,1,0:T(8,128)(2,1)}, bf16[2,2,128,128]{3,2,1,0:T(8,128)(2,1)S(1)}, u32[]{:S(2)}) copy-start(bf16[2,2,128,128]{3,2,1,0:T(8,128)(2,1)S(1)} %collective-permute-done.8.refs_5_) | copy-start | bytes 393220
  48.9 4.9 %collective-permute-start.10 = (bf16[1,2,128,128]{3,2,1,0:T(8,128)(2,1)S(1)}, bf16[1,2,128,128]{3,2,1,0:T(8,128)(2,1)}, u32[]{:S(2)}, u32[]{:S(2)}) collective-permute-start(bf16[1,2,128,128]{3,2,1,0:T(8,128)(2,1)S(1)} %slice.42), channel_id=1, source_target_pairs={{0,4},{1,5},{2,6},{3,7},{4,8},{5,9},{6,10},{7,11},{8,12},{9,13},{1... | collective-permute-start | bytes 196616 | tf_op jit(solution)/shard_map/ppermute | solution.py:346
  49.0 5.6 %copy-start.5 = (bf16[2,2,128,128]{3,2,1,0:T(8,128)(2,1)}, bf16[2,2,128,128]{3,2,1,0:T(8,128)(2,1)S(1)}, u32[]{:S(2)}) copy-start(bf16[2,2,128,128]{3,2,1,0:T(8,128)(2,1)S(1)} %collective-permute-done.9.refs_6_) | copy-start | bytes 393220
  49.7 4.9 %collective-permute-start.11 = (bf16[1,2,128,128]{3,2,1,0:T(8,128)(2,1)}, bf16[1,2,128,128]{3,2,1,0:T(8,128)(2,1)}, u32[]{:S(2)}, u32[]{:S(2)}) collective-permute-start(bf16[1,2,128,128]{3,2,1,0:T(8,128)(2,1)} %slice.43), channel_id=1, source_target_pairs={{0,28},{1,29},{2,30},{3,31},{4,0},{5,1},{6,2},{7,3},{8,4},{9,5},{1... | collective-permute-start | bytes 196616 | tf_op jit(solution)/shard_map/ppermute | solution.py:346
  57.1 12.3 %collective-permute-start.12 = (bf16[6,2,128,128]{3,2,1,0:T(8,128)(2,1)}, bf16[6,2,128,128]{3,2,1,0:T(8,128)(2,1)S(1)}, u32[]{:S(2)}, u32[]{:S(2)}) collective-permute-start(bf16[6,2,128,128]{3,2,1,0:T(8,128)(2,1)} %get-tuple-element.12), channel_id=1, source_target_pairs={{0,1},{1,2},{2,3},{3,0},{4,5},{5,6},{6,7},{7,4},{8,9},{9,10},{10,1... | collective-permute-start | bytes 1179656 | tf_op jit(solution)/shard_map/ppermute | solution.py:353
  59.0 10.6 %collective-permute-start.13 = (bf16[6,2,128,128]{3,2,1,0:T(8,128)(2,1)}, bf16[6,2,128,128]{3,2,1,0:T(8,128)(2,1)S(1)}, u32[]{:S(2)}, u32[]{:S(2)}) collective-permute-start(bf16[6,2,128,128]{3,2,1,0:T(8,128)(2,1)} %get-tuple-element.12), channel_id=1, source_target_pairs={{0,3},{1,0},{2,1},{3,2},{4,7},{5,4},{6,5},{7,6},{8,11},{9,8},{10,9... | collective-permute-start | bytes 1179656 | tf_op jit(solution)/shard_map/ppermute | solution.py:353
  66.6 15.3 %copy-start.11 = (s32[64]{0:T(128)S(1)}, s32[64]{0:T(128)}, u32[]{:S(2)}) copy-start(s32[64]{0:T(128)} %param.15) | copy-start | bytes 772
  69.5 11.2 %collective-permute-start.14 = (bf16[3,2,128,128]{3,2,1,0:T(8,128)(2,1)S(1)}, bf16[3,2,128,128]{3,2,1,0:T(8,128)(2,1)S(1)}, u32[]{:S(2)}, u32[]{:S(2)}) collective-permute-start(bf16[3,2,128,128]{3,2,1,0:T(8,128)(2,1)S(1)} %slice.44), channel_id=1, source_target_pairs={{0,1},{1,2},{2,3},{3,0},{4,5},{5,6},{6,7},{7,4},{8,9},{9,10},{10,1... | collective-permute-start | bytes 589832 | tf_op jit(solution)/shard_map/ppermute | solution.py:353
  69.6 11.1 %collective-permute-start.15 = (bf16[3,2,128,128]{3,2,1,0:T(8,128)(2,1)S(1)}, bf16[3,2,128,128]{3,2,1,0:T(8,128)(2,1)S(1)}, u32[]{:S(2)}, u32[]{:S(2)}) collective-permute-start(bf16[3,2,128,128]{3,2,1,0:T(8,128)(2,1)S(1)} %slice.45), channel_id=1, source_target_pairs={{0,3},{1,0},{2,1},{3,2},{4,7},{5,4},{6,5},{7,6},{8,11},{9,8},{10,9... | collective-permute-start | bytes 589832 | tf_op jit(solution)/shard_map/ppermute | solution.py:353
  80.7 1.1 copy-start
  140.2 1.4 copy-start.1
  158.9 5.6 %copy-start.2 = (bf16[2,1024,128]{2,1,0:T(8,128)(2,1)S(1)}, bf16[2,1024,128]{2,1,0:T(8,128)(2,1)}, u32[]{:S(2)}) copy-start(bf16[2,1024,128]{2,1,0:T(8,128)(2,1)} %kv_ref.3) | copy-start | bytes 1572868
  159.0 5.6 %copy-start.3 = (bf16[1024,1024]{1,0:T(8,128)(2,1)S(1)}, bf16[1024,1024]{1,0:T(8,128)(2,1)}, u32[]{:S(2)}) copy-start(bf16[1024,1024]{1,0:T(8,128)(2,1)} %q_ref.2) | copy-start | bytes 6291460
  159.0 31.9 %all-to-all-start.1 = ((bf16[8,1024,128]{2,1,0:T(8,128)(2,1)}), bf16[8,1024,128]{2,1,0:T(8,128)(2,1)}, u32[]{:S(2)}, u32[]{:S(2)}) async-start(bf16[8,1024,128]{2,1,0:T(8,128)(2,1)} %shard_map.117), calls=%async_computation.1 | async-start | bytes 4194304 | tf_op jit(solution)/shard_map/all_to_all | solution.py:464
Sparse Core Ops, SparseCore 0:
  11.1 128.9 all-gather.1
